TPU v7x, 128 devices: a whole 4x4x4 slice. The times are simulated.
128 devices in a mesh: seg: 8 (over y, z_lo), space: 16 (over x, z_hi, core).
Axes of the slice: x: 4, y: 4, z: 4 (z_hi: 2, z_lo: 2; z = z_hi * 2 + z_lo), core: 2. Of those that a mesh axis runs over, the one named last changes fastest.
Arguments:
- vorticity: float32 [8, 2048, 2048], P('seg', 'space'), may hold values from -6 to 6
Outputs:
- gradient: float32 [8, 2048, 2048], P('seg', 'space')
- residual_spectrum: float32 [8, 2, 2048, 2048], P('seg', None, None, 'space')
All inputs are finite; a program needn't handle non-finite values.
Results may differ from a plain program's by a relative error of at most 0.0001.
Values sent between devices are 32-bit elements; how exact they have to be, the bound alone decides.
A program may use at most 128 MiB of HBM per device.

v0:
```python
import math

import jax
import jax.numpy as jnp
from jax import lax
from jax.sharding import PartitionSpec as P

time_step = 0.3
drag_rate = 0.05
force_amp = 0.8
forcing_wave = 4
high_prec = lax.Precision.HIGHEST


def exchange_in_groups(value, axis, split_dim, concat_dim, work, item_dim, out_dim):
    items = jax.tree.leaves(value)[0].shape[item_dim]
    count = 2 if items % 2 == 0 else 1
    outs = []
    for k in range(count):
        group = jax.tree.map(
            lambda a: lax.slice_in_dim(
                a, k * (items // count), (k + 1) * (items // count), axis=item_dim
            ),
            value,
        )
        outs.append(
            work(
                lax.all_to_all(
                    group, axis, split_axis=split_dim, concat_axis=concat_dim, tiled=True
                )
            )
        )
    return jax.tree.map(lambda *parts: jnp.concatenate(parts, axis=out_dim), *outs)


def from_behind(block, axis, distance):
    devices = range(lax.axis_size(axis))
    route = [((i - distance) % len(devices), i) for i in devices]
    return lax.ppermute(block, axis, route)


def angle_table(row_count, col_count, modulus, sign_value):
    row_iota = lax.broadcasted_iota(jnp.int32, (row_count, col_count), 0)
    col_iota = lax.broadcasted_iota(jnp.int32, (row_count, col_count), 1)
    phase_index = row_iota * col_iota % modulus
    return sign_value * 2.0 * math.pi * phase_index.astype(jnp.float32) / modulus


def twisted_angles(large_len, small_len, length, sign_value):
    shape_now = (large_len, large_len, small_len)
    b_iota = lax.broadcasted_iota(jnp.int32, shape_now, 0)
    k_iota = lax.broadcasted_iota(jnp.int32, shape_now, 1)
    a_iota = lax.broadcasted_iota(jnp.int32, shape_now, 2)
    phase_index = k_iota * (b_iota * small_len + a_iota) % length
    return sign_value * 2.0 * math.pi * phase_index.astype(jnp.float32) / length


def block_table(angles, factor):
    real_part = jnp.cos(angles) * factor
    imag_part = jnp.sin(angles) * factor
    upper_half = jnp.stack([real_part, imag_part], axis=1)
    lower_half = jnp.stack([-imag_part, real_part], axis=1)
    return jnp.stack([upper_half, lower_half], axis=0)


def fourier_tables(length, sign_value, factor):
    small_len = 2 ** (length.bit_length() // 2)
    large_len = length // small_len
    inner_table = block_table(twisted_angles(large_len, small_len, length, sign_value), 1.0)
    outer_table = block_table(angle_table(small_len, small_len, small_len, sign_value), factor)
    return (small_len, large_len, inner_table, outer_table)


def transform_last(values, tables):
    small_len, large_len, inner_table, outer_table = tables
    part_count, field_count, row_count, length = values.shape
    grid_view = values.reshape(part_count, field_count, row_count, large_len, small_len)
    middle = jnp.einsum("pfrba,pbqka->qfrka", grid_view, inner_table, precision=high_prec)
    result = jnp.einsum("pfrka,paqj->qfrjk", middle, outer_table, precision=high_prec)
    return result.reshape(part_count, field_count, row_count, length)


def transform_middle(values, tables):
    small_len, large_len, inner_table, outer_table = tables
    part_count, field_count, length, col_count = values.shape
    grid_view = values.reshape(part_count, field_count, large_len, small_len, col_count)
    middle = jnp.einsum("pfbac,pbqka->qfkac", grid_view, inner_table, precision=high_prec)
    result = jnp.einsum("pfkac,paqj->qfjkc", middle, outer_table, precision=high_prec)
    return result.reshape(part_count, field_count, length, col_count)


def to_layout(values, slab_count):
    leading = values.shape[:-1]
    length = values.shape[-1]
    half_len = length // 2
    group = half_len // slab_count
    lower = values[..., :half_len].reshape(leading + (slab_count, group))
    mirrored = jnp.concatenate(
        [values[..., half_len : half_len + 1], jnp.flip(values[..., half_len + 1 :], -1)], -1
    )
    upper = mirrored.reshape(leading + (slab_count, group))
    return jnp.stack([lower, upper], -2).reshape(leading + (length,))


def from_layout(values, slab_count):
    leading = values.shape[:-1]
    length = values.shape[-1]
    half_len = length // 2
    group = half_len // slab_count
    grouped = values.reshape(leading + (slab_count, 2, group))
    lower = grouped[..., 0, :].reshape(leading + (half_len,))
    upper = grouped[..., 1, :].reshape(leading + (half_len,))
    return jnp.concatenate([lower, upper[..., :1], jnp.flip(upper[..., 1:], -1)], -1)


def to_spectral(values, forward_tab):
    lines = to_layout(transform_last(values, forward_tab), lax.axis_size("space"))
    return exchange_in_groups(
        lines, "space", 3, 2, lambda pieces: transform_middle(pieces, forward_tab), 1, 1
    )


def to_physical(values, inverse_tab):
    slab_count = lax.axis_size("space")
    columns = transform_middle(values, inverse_tab)
    return (lambda pieces: transform_last(from_layout(pieces, slab_count), inverse_tab))(
        lax.all_to_all(columns, "space", split_axis=2, concat_axis=3, tiled=True)
    )


def wave_tables(length, col_count, device):
    half_cols = col_count // 2
    kx_index = lax.broadcasted_iota(jnp.int32, (length, col_count), 0)
    slot = lax.broadcasted_iota(jnp.int32, (length, col_count), 1)
    lower = device * half_cols + slot
    upper = length - device * half_cols - (slot - half_cols)
    upper = jnp.where(upper == length, length // 2, upper)
    ky_index = jnp.where(slot < half_cols, lower, upper)
    half_len = length // 2
    kx_wave = jnp.where(kx_index < half_len, kx_index, kx_index - length)
    ky_wave = jnp.where(ky_index < half_len, ky_index, ky_index - length)
    kx_deriv = jnp.where(kx_index == half_len, 0, kx_wave).astype(jnp.float32)
    ky_deriv = jnp.where(ky_index == half_len, 0, ky_wave).astype(jnp.float32)
    kx_float = kx_wave.astype(jnp.float32)
    ky_float = ky_wave.astype(jnp.float32)
    wave_sq = kx_float * kx_float + ky_float * ky_float
    inv_sq = jnp.where(wave_sq > 0, 1.0 / jnp.maximum(wave_sq, 1.0), 0.0)
    decay_fac = jnp.exp(-time_step * (drag_rate + 9.0 * wave_sq / (length * length)))
    keep_mask = ((3 * jnp.abs(kx_wave) <= length) & (3 * jnp.abs(ky_wave) <= length)).astype(
        jnp.float32
    )
    nl_factor = time_step * decay_fac * keep_mask
    at_force = (kx_index == 0) & ((ky_index == forcing_wave) | (ky_index == length - forcing_wave))
    force_hat = jnp.where(
        at_force, time_step * decay_fac * force_amp * (length * length / 2.0), 0.0
    )
    return (kx_deriv, ky_deriv, inv_sq, decay_fac, nl_factor, force_hat)


def pair_pack(spec_re, spec_im, coeff_one, coeff_two):
    return jnp.stack(
        [-coeff_one * spec_im - coeff_two * spec_re, coeff_one * spec_re - coeff_two * spec_im]
    )


def rotate(spectrum, real_coeff, imag_coeff):
    return jnp.stack(
        [
            real_coeff * spectrum[0] - imag_coeff * spectrum[1],
            real_coeff * spectrum[1] + imag_coeff * spectrum[0],
        ]
    )


def advance(spectrum, tables, inverse_tab, forward_tab):
    kx_deriv, ky_deriv, inv_sq, decay_fac, nl_factor, force_hat = tables
    spec_re, spec_im = (spectrum[0], spectrum[1])
    pack_velocity = pair_pack(spec_re, spec_im, ky_deriv * inv_sq, -kx_deriv * inv_sq)
    pack_gradient = pair_pack(spec_re, spec_im, kx_deriv, ky_deriv)
    physical = to_physical(jnp.stack([pack_velocity, pack_gradient], axis=1), inverse_tab)
    vel_x, vel_y = (physical[0, 0], physical[1, 0])
    grad_x, grad_y = (physical[0, 1], physical[1, 1])
    nonlinear = vel_x * grad_x + vel_y * grad_y
    nl_spec = to_spectral(jnp.stack([nonlinear, jnp.zeros_like(nonlinear)])[:, None], forward_tab)[
        :, 0
    ]
    advanced = decay_fac * spectrum - nl_factor * nl_spec
    advanced = advanced + jnp.stack([force_hat, jnp.zeros_like(force_hat)])
    return (advanced, (vel_x, vel_y, grad_x, grad_y))


def retreat(adjoint, stored, tables, inverse_tab, forward_tab):
    kx_deriv, ky_deriv, inv_sq, decay_fac, nl_factor, force_hat = tables
    vel_x, vel_y, grad_x, grad_y = stored
    weight = to_physical((nl_factor * adjoint)[:, None], inverse_tab)[0, 0]
    carried = decay_fac * adjoint
    packed = jnp.stack(
        [jnp.stack([weight * vel_x, weight * grad_x]), jnp.stack([weight * vel_y, weight * grad_y])]
    )
    spectra = to_spectral(packed, forward_tab)
    term_one = rotate(spectra[:, 0], ky_deriv, kx_deriv)
    term_two = rotate(spectra[:, 1], -kx_deriv * inv_sq, ky_deriv * inv_sq)
    combined = carried + term_one + term_two
    return combined


def body(vorticity):
    length = vorticity.shape[2]
    col_count = length // lax.axis_size("space")
    device = lax.axis_index("space")
    forward_tab = fourier_tables(length, -1.0, 1.0)
    inverse_tab = fourier_tables(length, 1.0, 1.0 / length)
    tables = wave_tables(length, col_count, device)
    initial = vorticity[0]
    start_spec = to_spectral(jnp.stack([initial, jnp.zeros_like(initial)])[:, None], forward_tab)[
        :, 0
    ]
    next_start = from_behind(start_spec, "seg", -1)
    end_spec = start_spec
    end_spec, stored = advance(end_spec, tables, inverse_tab, forward_tab)
    previous_end = from_behind(end_spec, "seg", 1)
    residual = previous_end - start_spec
    adjoint_seed = end_spec - next_start
    adjoint = adjoint_seed
    adjoint = retreat(adjoint, stored, tables, inverse_tab, forward_tab)
    gradient = to_physical((adjoint - residual)[:, None], inverse_tab)[0, 0]
    return (gradient[None], (residual / length)[None])


def solution(mesh):
    return jax.shard_map(
        body,
        mesh=mesh,
        in_specs=(P("seg", "space", None),),
        out_specs=(P("seg", "space", None), P("seg", None, None, "space")),
        check_vma=False,
    )
```

profile of v0, /device:TPU:1, one launch (start us, length us, event | category | flops | bytes accessed | tf_op | source)
XLA Modules:
  0.0 704.9 jit_solution(9058101309598357698)
XLA Ops:
  0.9 8.9 %multiply_sine_fusion.1 = (f32[32,1,32,64]{0,2,1,3:T(8,128)S(1)}, f32[32,1,32,64]{0,2,1,3:T(8,128)}, f32[32,1,32,64]{0,2,1,3:T(8,128)}, f32[32,1,32,64]{0,2,1,3:...) fusion(s32[32]{0:T(128)S(1)} %iota_multiply_fusion), kind=kLoop, calls=%fused_computation.195 | loop fusion | flops 1179648 | bytes 1572992 | tf_op jit(solution)/shard_map/sin | solution.py:60
  12.7 5.0 fusion.106
  17.8 3.0 fusion.109
  24.2 9.1 %rev.20 = f32[2,1,128,1023]{2,3,0,1:T(8,128)} reverse(f32[2,1,128,1023]{2,3,0,1:T(8,128)} %slice.154), dimensions={3} | reverse | bytes 2095104 | tf_op jit(solution)/shard_map/jit(_flip)/rev | solution.py:99
  35.3 8.9 %copy.178 = f32[2,1,128,2048]{2,0,1,3:T(2,128)} copy(f32[2,1,128,2048]{2,3,0,1:T(8,128)S(1)} %bitcast.435) | data formatting | bytes 4194304 | tf_op jit(solution)/shard_map/reshape | solution.py:102
  44.2 9.1 %all-to-all-start = ((f32[2,1,128,2048]{2,0,1,3:T(2,128)}), f32[2,1,128,2048]{2,0,1,3:T(2,128)}, u32[]{:S(2)}, u32[]{:S(2)}) async-start(f32[2,1,128,2048]{2,0,1,3:T(2,128)} %copy.178), calls=%async_computation | async-start | bytes 4194304 | tf_op jit(solution)/shard_map/all_to_all | solution.py:28
  58.0 4.4 pad_maximum_fusion
  62.4 19.5 %all-to-all-done = f32[2,1,128,2048]{2,0,1,3:T(2,128)} async-done(((f32[2,1,128,2048]{2,0,1,3:T(2,128)}), f32[2,1,128,2048]{2,0,1,3:T(2,128)}, u32[]{:S(2)}, u32[]{:S(2)}) %all-to-all-start) | async-done | bytes 2097184 | tf_op jit(solution)/shard_map/all_to_all | solution.py:28
  81.9 3.0 copy.179
  87.8 7.2 %fusion.112 = f32[2,32,64,128]{3,1,0,2:T(8,128)S(1)} fusion(f32[2,32,64,128,1]{3,2,1,0,4:T(8,128)} %bitcast.449, f32[1,32,2,32,64]{1,3,0,2,4:T(8,128)} %copy-done, f32[1,32,2,32,64]{1,3,0,2,4:T(8,128)S(1)} %get-tuple-element.47), kind=kOutput, calls=%fused_computation.112 | convolution fusion | flops 402915328 | bytes 5242880 | tf_op jit(solution)/shard_map/pfbac,pbqka->qfkac/dot_general | solution.py:87
  102.9 5.2 fusion.53
  108.1 5.9 fusion.36
  116.9 10.5 %copy.198 = f32[2,2,2048,128]{3,1,0,2:T(2,128)S(1)} copy(f32[2,2,2048,128]{3,2,1,0:T(8,128)S(1)} %bitcast.419) | data formatting | bytes 8388608 | tf_op jit(solution)/shard_map/reshape | solution.py:89
  127.4 55.9 %all_to_all.105 = f32[2,2,2048,128]{3,1,0,2:T(2,128)S(1)} all-to-all(f32[2,2,2048,128]{3,1,0,2:T(2,128)S(1)} %copy.198), channel_id=1, replica_groups=mesh['seg'=8,'space'=16] {'space'}, dimensions={2} | all-to-all | bytes 8388608 | tf_op jit(solution)/shard_map/all_to_all | solution.py:127
  185.5 5.4 copy.200
  190.9 4.0 fusion.232
  196.4 17.1 %rev.21 = f32[2,2,128,1023]{2,3,1,0:T(8,128)} reverse(f32[2,2,128,1023]{2,3,1,0:T(8,128)} %slice.160), dimensions={3} | reverse | bytes 4190208 | tf_op jit(solution)/shard_map/jit(_flip)/rev | solution.py:113
  213.5 13.9 %concatenate.25 = f32[2,2,128,2048]{2,3,1,0:T(8,128)} concatenate(f32[2,2,128,1024]{2,3,1,0:T(8,128)} %bitcast.430, f32[2,2,128,1]{2,3,1,0:T(1,128)S(1)} %slice.159, f32[2,2,128,1023]{2,3,1,0:T(8,128)} %rev.21), dimensions={3} | concatenate | bytes 8388608 | tf_op jit(solution)/shard_map/concatenate | solution.py:113
  227.4 10.7 %fusion.39 = f32[2,2,128,32,64]{2,3,1,0,4:T(8,128)S(1)} fusion(f32[2,2,128,32,64,1]{2,4,3,1,0,5:T(8,128)} %bitcast.415, f32[2,32,2,32,64,1]{1,3,2,4,0,5:T(8,128)} %get-tuple-element.20), kind=kOutput, calls=%fused_computation.45 | convolution fusion | flops 805306368 | bytes 9437184 | tf_op jit(solution)/shard_map/pfrba,pbqka->qfrka/dot_general | solution.py:78
  238.1 6.3 fusion.44
  250.5 5.0 fusion.118
  255.5 3.2 fusion.121
  261.2 5.3 rev.22
  268.5 8.6 %copy.210 = f32[2,1,128,2048]{2,0,1,3:T(2,128)} copy(f32[2,1,128,2048]{2,3,0,1:T(8,128)S(1)} %bitcast.437) | data formatting | bytes 4194304 | tf_op jit(solution)/shard_map/reshape | solution.py:102
  277.1 5.5 all-to-all-start.2
  282.7 4.2 copy.183
  286.9 3.2 collective-permute-start
  295.5 58.7 %all-to-all-done.2 = f32[2,1,128,2048]{2,0,1,3:T(2,128)} async-done(((f32[2,1,128,2048]{2,0,1,3:T(2,128)}), f32[2,1,128,2048]{2,0,1,3:T(2,128)}, u32[]{:S(2)}, u32[]{:S(2)}) %all-to-all-start.2) | async-done | bytes 2097184 | tf_op jit(solution)/shard_map/all_to_all | solution.py:28
  354.2 3.0 copy.211
  357.3 3.3 copy.212
  360.5 7.2 %fusion.124 = f32[2,32,64,128]{3,1,0,2:T(8,128)S(1)} fusion(f32[2,32,64,128,1]{3,2,1,0,4:T(8,128)} %bitcast.450, f32[1,32,2,32,64]{1,3,0,2,4:T(8,128)} %copy-done, f32[1,32,2,32,64]{1,3,0,2,4:T(8,128)S(1)} %get-tuple-element.47), kind=kOutput, calls=%fused_computation.116 | convolution fusion | flops 402915328 | bytes 5242880 | tf_op jit(solution)/shard_map/pfbac,pbqka->qfkac/dot_general | solution.py:87
  367.7 3.0 fusion.127
  372.3 4.1 broadcast_multiply_fusion
  376.4 5.2 fusion.154
  385.9 7.6 %copy.220 = f32[2,1,2048,128]{3,0,1,2:T(2,128)S(1)} copy(f32[2,1,2048,128]{3,2,0,1:T(8,128)S(1)} %bitcast.439) | data formatting | bytes 4194304 | tf_op jit(solution)/shard_map/reshape;pfkac,paqj->qfjkc/transpose | solution.py:89
  393.5 32.8 %all_to_all.106 = f32[2,1,2048,128]{3,0,1,2:T(2,128)S(1)} all-to-all(f32[2,1,2048,128]{3,0,1,2:T(2,128)S(1)} %copy.220), channel_id=1, replica_groups=mesh['seg'=8,'space'=16] {'space'}, dimensions={2} | all-to-all | bytes 4194304 | tf_op jit(solution)/shard_map/all_to_all | solution.py:127
  434.5 9.1 %rev.23 = f32[2,1,128,1023]{2,3,0,1:T(8,128)} reverse(f32[2,1,128,1023]{2,3,0,1:T(8,128)} %slice.171), dimensions={3} | reverse | bytes 2095104 | tf_op jit(solution)/shard_map/jit(_flip)/rev | solution.py:113
  443.6 8.7 %concatenate.27 = f32[2,1,128,2048]{2,3,0,1:T(8,128)} concatenate(f32[2,1,128,1024]{2,3,0,1:T(8,128)} %bitcast.463, f32[2,1,128,1]{2,3,0,1:T(1,128)S(1)} %slice.170, f32[2,1,128,1023]{2,3,0,1:T(8,128)} %rev.23), dimensions={3} | concatenate | bytes 4194304 | tf_op jit(solution)/shard_map/concatenate | solution.py:113
  452.3 7.8 %fusion.159 = f32[2,128,32,64]{1,2,3,0:T(8,128)S(1)} fusion(f32[2,128,32,64,1]{1,3,2,0,4:T(8,128)} %bitcast.433, f32[2,32,2,32,64]{1,3,2,4,0:T(8,128)} %get-tuple-element.19), kind=kOutput, calls=%fused_computation.127 | convolution fusion | flops 402653184 | bytes 5242880 | tf_op jit(solution)/shard_map/pfrba,pbqka->qfrka/dot_general | solution.py:78
  460.2 3.0 fusion.133
  465.4 3.1 copy_multiply_fusion.3
  468.6 5.1 fusion.50
  473.7 5.9 fusion.47
  485.2 17.1 %rev.24 = f32[2,2,128,1023]{2,3,1,0:T(8,128)} reverse(f32[2,2,128,1023]{2,3,1,0:T(8,128)} %slice.175), dimensions={3} | reverse | bytes 4190208 | tf_op jit(solution)/shard_map/jit(_flip)/rev | solution.py:99
  507.4 9.9 %copy.238 = f32[2,1,128,2048]{2,1,0,3:T(1,128)} copy(f32[2,1,128,2048]{2,3,1,0:T(8,128)S(1)} %get-tuple-element.13) | data formatting | bytes 4194304 | tf_op jit(solution)/shard_map/slice | solution.py:21
  517.3 5.5 all-to-all-start.4
  522.8 4.8 copy.245
  527.6 23.8 %all-to-all-done.4 = f32[2,1,128,2048]{2,1,0,3:T(1,128)} async-done(((f32[2,1,128,2048]{2,1,0,3:T(1,128)}), f32[2,1,128,2048]{2,1,0,3:T(1,128)}, u32[]{:S(2)}, u32[]{:S(2)}) %all-to-all-start.4) | async-done | bytes 2097184 | tf_op jit(solution)/shard_map/all_to_all | solution.py:28
  551.4 5.5 all-to-all-start.5
  557.0 3.1 copy.239
  560.1 3.3 copy.240
  563.4 7.2 %fusion.136 = f32[2,32,64,128]{3,1,0,2:T(8,128)S(1)} fusion(f32[2,32,64,128,1]{3,2,1,0,4:T(8,128)} %bitcast.451, f32[1,32,2,32,64]{1,3,0,2,4:T(8,128)} %copy-done, f32[1,32,2,32,64]{1,3,0,2,4:T(8,128)S(1)} %get-tuple-element.47), kind=kOutput, calls=%fused_computation.120 | convolution fusion | flops 402915328 | bytes 5242880 | tf_op jit(solution)/shard_map/pfbac,pbqka->qfkac/dot_general | solution.py:87
  570.6 3.0 fusion.139
  577.0 8.5 %all-to-all-done.5 = f32[2,1,128,2048]{2,1,0,3:T(1,128)} async-done(((f32[2,1,128,2048]{2,1,0,3:T(1,128)}), f32[2,1,128,2048]{2,1,0,3:T(1,128)}, u32[]{:S(2)}, u32[]{:S(2)}) %all-to-all-start.5) | async-done | bytes 2097184 | tf_op jit(solution)/shard_map/all_to_all | solution.py:28
  585.5 3.1 copy.246
  588.6 3.1 copy.247
  591.7 7.2 %fusion.142 = f32[2,32,64,128]{3,1,0,2:T(8,128)S(1)} fusion(f32[2,32,64,128,1]{3,2,1,0,4:T(8,128)} %bitcast.447, f32[1,32,2,32,64]{1,3,0,2,4:T(8,128)} %copy-done, f32[1,32,2,32,64]{1,3,0,2,4:T(8,128)S(1)} %get-tuple-element.47), kind=kOutput, calls=%fused_computation.122 | convolution fusion | flops 402915328 | bytes 5242880 | tf_op jit(solution)/shard_map/pfbac,pbqka->qfkac/dot_general | solution.py:87
  606.2 18.7 %collective-permute-done.1 = f32[2,2048,128]{2,1,0:T(8,128)} collective-permute-done((f32[2,2048,128]{2,1,0:T(8,128)}, f32[2,2048,128]{2,1,0:T(8,128)}, u32[]{:S(2)}, u32[]{:S(2)}) %collective-permute-start.1) | collective-permute-done | bytes 2097184 | tf_op jit(solution)/shard_map/ppermute | solution.py:39
  624.9 5.3 multiply_bitcast_fusion
  630.2 5.0 fusion.164
  639.5 7.8 %copy.256 = f32[2,1,2048,128]{3,0,1,2:T(2,128)S(1)} copy(f32[2,1,2048,128]{3,2,0,1:T(8,128)S(1)} %bitcast.443) | data formatting | bytes 4194304 | tf_op jit(solution)/shard_map/reshape;pfkac,paqj->qfjkc/transpose | solution.py:89
  647.4 35.3 %all_to_all.107 = f32[2,1,2048,128]{3,0,1,2:T(2,128)S(1)} all-to-all(f32[2,1,2048,128]{3,0,1,2:T(2,128)S(1)} %copy.256), channel_id=1, replica_groups=mesh['seg'=8,'space'=16] {'space'}, dimensions={2} | all-to-all | bytes 4194304 | tf_op jit(solution)/shard_map/all_to_all | solution.py:127
  688.4 4.0 concatenate.29
  692.4 7.0 fusion.169
  (154 shorter events, 98.7 us)
Async XLA Ops:
  0.9 8.9 %copy-start.22 = (f32[1,128,2048]{2,1,0:T(8,128)S(1)}, f32[1,128,2048]{2,1,0:T(8,128)}, u32[]{:S(2)}) copy-start(f32[1,128,2048]{2,1,0:T(8,128)} %param.1) | copy-start | bytes 3145732
  10.2 1.2 copy-start.13
  10.2 1.5 copy-start.14
  10.2 1.8 copy-start.15
  12.7 5.1 copy-start
  33.3 1.5 copy-start.18
  44.2 37.7 %all-to-all-start = ((f32[2,1,128,2048]{2,0,1,3:T(2,128)}), f32[2,1,128,2048]{2,0,1,3:T(2,128)}, u32[]{:S(2)}, u32[]{:S(2)}) async-start(f32[2,1,128,2048]{2,0,1,3:T(2,128)} %copy.178), calls=%async_computation | async-start | bytes 4194304 | tf_op jit(solution)/shard_map/all_to_all | solution.py:28
  98.0 1.3 copy-start.6
  99.4 1.3 copy-start.23
  99.4 1.3 copy-start.24
  99.4 1.3 copy-start.25
  99.4 1.3 copy-start.27
  99.4 1.3 copy-start.29
  99.4 1.3 copy-start.31
  100.7 2.2 copy-start.5
  248.9 1.6 copy-start.1
  266.5 1.5 copy-start.19
  277.1 77.1 %all-to-all-start.2 = ((f32[2,1,128,2048]{2,0,1,3:T(2,128)}), f32[2,1,128,2048]{2,0,1,3:T(2,128)}, u32[]{:S(2)}, u32[]{:S(2)}) async-start(f32[2,1,128,2048]{2,0,1,3:T(2,128)} %copy.210), calls=%async_computation.2 | async-start | bytes 4194304 | tf_op jit(solution)/shard_map/all_to_all | solution.py:28
  282.6 7.4 %copy-start.26 = (s32[128]{0:T(128)S(1)}, s32[128]{0:T(128)}, u32[]{:S(2)}) copy-start(s32[128]{0:T(128)} %get-tuple-element.65) | copy-start | bytes 1540
  282.6 7.4 %copy-start.28 = (s32[128]{0:T(128)S(1)}, s32[128]{0:T(128)}, u32[]{:S(2)}) copy-start(s32[128]{0:T(128)} %get-tuple-element.66) | copy-start | bytes 1540
  282.7 7.4 %copy-start.30 = (pred[128]{0:T(512)(128)(4,1)S(1)}, pred[128]{0:T(512)(128)(4,1)}, u32[]{:S(2)}) copy-start(pred[128]{0:T(512)(128)(4,1)} %get-tuple-element.67) | copy-start | bytes 388
  282.7 7.4 %copy-start.32 = (pred[128]{0:T(512)(128)(4,1)S(1)}, pred[128]{0:T(512)(128)(4,1)}, u32[]{:S(2)}) copy-start(pred[128]{0:T(512)(128)(4,1)} %get-tuple-element.68) | copy-start | bytes 388
  286.9 85.2 %collective-permute-start = (f32[2,2048,128]{2,1,0:T(8,128)}, f32[2,2048,128]{2,1,0:T(8,128)}, u32[]{:S(2)}, u32[]{:S(2)}) collective-permute-start(f32[2,2048,128]{2,1,0:T(8,128)} %bitcast.43), channel_id=1, source_target_pairs={{16,0},{32,16},{48,32},{64,48},{80,64},{96,80},{112,96},{0,112},{1... | collective-permute-start | bytes 6291464 | tf_op jit(solution)/shard_map/ppermute | solution.py:39
  370.8 1.3 copy-start.20
  370.8 1.5 copy-start.21
  372.3 4.1 copy-start.3
  463.2 1.2 copy-start.9
  463.2 1.5 copy-start.10
  463.2 1.8 copy-start.11
  463.2 2.1 copy-start.12
  465.4 3.1 copy-start.2
  502.4 2.2 copy-start.8
  517.3 34.1 %all-to-all-start.4 = ((f32[2,1,128,2048]{2,1,0,3:T(1,128)}), f32[2,1,128,2048]{2,1,0,3:T(1,128)}, u32[]{:S(2)}, u32[]{:S(2)}) async-start(f32[2,1,128,2048]{2,1,0,3:T(1,128)} %copy.238), calls=%async_computation.4 | async-start | bytes 4194304 | tf_op jit(solution)/shard_map/all_to_all | solution.py:28
  551.4 34.1 %all-to-all-start.5 = ((f32[2,1,128,2048]{2,1,0,3:T(1,128)}), f32[2,1,128,2048]{2,1,0,3:T(1,128)}, u32[]{:S(2)}, u32[]{:S(2)}) async-start(f32[2,1,128,2048]{2,1,0,3:T(1,128)} %copy.245), calls=%async_computation.5 | async-start | bytes 4194304 | tf_op jit(solution)/shard_map/all_to_all | solution.py:28
  556.9 68.0 %collective-permute-start.1 = (f32[2,2048,128]{2,1,0:T(8,128)}, f32[2,2048,128]{2,1,0:T(8,128)}, u32[]{:S(2)}, u32[]{:S(2)}) collective-permute-start(f32[2,2048,128]{2,1,0:T(8,128)} %get-tuple-element.9), channel_id=1, source_target_pairs={{112,0},{0,16},{16,32},{32,48},{48,64},{64,80},{80,96},{96,112},{1... | collective-permute-start | bytes 6291464 | tf_op jit(solution)/shard_map/ppermute | solution.py:39
  602.1 1.3 copy-start.16
  602.1 1.5 copy-start.17
  603.6 21.3 %copy-start.7 = (f32[2,2048,128]{2,1,0:T(8,128)S(1)}, f32[2,2048,128]{2,1,0:T(8,128)}, u32[]{:S(2)}) copy-start(f32[2,2048,128]{2,1,0:T(8,128)} %get-tuple-element.9) | copy-start | bytes 6291460
  624.9 5.3 copy-start.4
where the time goes:
time: 719 us; the launch traced here: 705 us
  local copies, waits for them, and re-layouts  238 us (33%)
  matrix products  133 us (18%)
  waiting for transfers between devices  129 us (18%)
  blocking collectives  124 us (17%)
  other arithmetic  49 us (7%)
  starting transfers between devices  28.9 us (4%)
    all_to_all x3, blocking collectives, to_physical(): lax.all_to_all(columns, 'space', split_axis=2, concat_axis=3, tiled=True)  124 us
    all_to_all x4, waiting for transfers between devices, exchange_in_groups(): lax.all_to_all(group, axis, split_axis=split_dim, concat_axis=concat_dim,...  111 us
    dot_general x7, matrix products, transform_middle(): jnp.einsum('pfbac,pbqka->qfkac', grid_view, inner_table, precision=high_p...  44.3 us
    dot_general x6, matrix products, transform_last(): jnp.einsum('pfrba,pbqka->qfrka', grid_view, inner_table, precision=high_p...  40.8 us
    rev x3, local copies, waits for them, and re-layouts, to_layout(): jnp.flip(values[..., half_len + 1:], -1)  31.6 us
    rev x3, local copies, waits for them, and re-layouts, from_layout(): jnp.flip(upper[..., 1:], -1)  27.4 us
    concatenate x3, local copies, waits for them, and re-layouts, from_layout(): jnp.concatenate([lower, upper[..., :1], jnp.flip(upper[..., 1:], -1)], -1)  26.6 us
    all_to_all x4, starting transfers between devices, exchange_in_groups(): lax.all_to_all(group, axis, split_axis=split_dim, concat_axis=concat_dim,...  25.6 us
  transfers between devices with their start and end apart: 6, of which 5 were waited for; matrix products, arithmetic and copies ran while one was open for 12% of the time, Pallas kernels for 0%

commit v1 on v0

v1 whole, which is shorter than its diff:
```python
import functools
import math

import jax
import jax.numpy as jnp
import ml_dtypes
import numpy as np
from jax import lax
from jax.experimental import pallas as pl
from jax.experimental.pallas import tpu as pltpu
from jax.sharding import PartitionSpec as P

N = 2048
SLABS = 16
LANES = 128
ROWS_KY = 72
PAIR = 2 * ROWS_KY
TIME_STEP = 0.3
DRAG = 0.05
FORCE_AMP = 0.8
FORCING_WAVE = 4
MESH = pl.DeviceIdType.MESH
F32 = jnp.float32
BF16 = jnp.bfloat16


def split_table(table):
    high = table.astype(np.float32).astype(ml_dtypes.bfloat16)
    low = (table - high.astype(np.float64)).astype(np.float32).astype(ml_dtypes.bfloat16)
    return high, low


def slot_wave(j, d, r):
    if r < 4:
        return j + 16 * (4 * d + r)
    return (16 - j if j else 8) + 16 * (4 * d + r - 4)


@functools.cache
def row_tables():
    a = np.arange(LANES)
    forward = np.zeros((8, 16, 2, 8, 2, LANES))
    inverse = np.zeros((8, 2, LANES, 16, 2, 8))
    wave = np.zeros((8, 16, 8))
    for j in range(8):
        for d in range(16):
            for r in range(8):
                k = slot_wave(j, d, r)
                wave[j, d, r] = k
                c = np.cos(2 * np.pi * ((a * k) % N) / N)
                s = np.sin(2 * np.pi * ((a * k) % N) / N)
                if j == 0:
                    part = 0 if r < 4 else 1
                    forward[j, d, 0, r, part] = c
                    forward[j, d, 1, r, part] = -s
                    inverse[j, part, :, d, 0, r] = 2 * c
                    inverse[j, part, :, d, 1, r] = -2 * s
                    if k == 0:
                        alternate = 1.0 - 2.0 * (a % 2)
                        forward[j, d, 1, r, part] = alternate
                        inverse[j, part, :, d, 0, r] = 1.0
                        inverse[j, part, :, d, 1, r] = alternate
                else:
                    sign = 1.0 if r < 4 else -1.0
                    forward[j, d, 0, r, 0] = c
                    forward[j, d, 0, r, 1] = sign * s
                    forward[j, d, 1, r, 0] = -s
                    forward[j, d, 1, r, 1] = sign * c
                    inverse[j, 0, :, d, 0, r] = c
                    inverse[j, 0, :, d, 1, r] = -s
                    inverse[j, 1, :, d, 0, r] = sign * s
                    inverse[j, 1, :, d, 1, r] = sign * c
    inverse /= N
    dwave = wave[:, :, None, :, None, None]
    forward_dy = np.stack([-forward[:, :, 1], forward[:, :, 0]], axis=2) * dwave
    inverse_dy = np.stack([inverse[..., 1, :], -inverse[..., 0, :]], axis=-2) * wave[:, None, None, :, None, :]
    shape = (8, 256, 256)
    outs = []
    for table in (forward, forward_dy, inverse, inverse_dy):
        high, low = split_table(table.reshape(shape))
        outs.append(np.stack([high, low]))
    return np.stack(outs)


@functools.cache
def col_tables():
    a = np.arange(LANES)
    angle = 2 * np.pi * (np.outer(a, a) % LANES) / LANES
    c, s = np.cos(angle), np.sin(angle)
    forward = np.block([[c, -s], [s, c]])
    inverse = np.block([[c, s], [-s, c]]) / N
    mats = np.stack([np.stack(split_table(m)) for m in (forward, inverse)])
    angle = 2 * np.pi * np.outer(np.arange(16), a) / N
    twiddle = np.stack([np.cos(angle), np.sin(angle)], axis=1)
    twiddle = np.broadcast_to(twiddle[:, :, None, :], (16, 2, 8, LANES)).astype(np.float32)
    return mats, np.ascontiguousarray(twiddle)


@functools.cache
def flip_tables():
    eye = np.eye(LANES)
    first = np.concatenate([eye, eye[(LANES - np.arange(LANES)) % LANES]], axis=1)
    other = np.concatenate([eye, eye[LANES - 1 - np.arange(LANES)]], axis=1)
    return (np.stack([first, other]) / N).astype(ml_dtypes.bfloat16)


@functools.cache
def slot_table():
    return np.array([[slot_wave(j, 0, r) for r in range(8)] for j in range(8)], np.int32)


def times_root(re, im, k, n, sign):
    k = k % n
    if im is None:
        if k == 0:
            return re, None
        angle = sign * 2 * math.pi * k / n
        if 4 * k == n:
            return None, (re if sign > 0 else -re)
        return re * math.cos(angle), re * math.sin(angle)
    if k == 0:
        return re, im
    if 2 * k == n:
        return -re, -im
    if 4 * k == n:
        return (-im, re) if sign > 0 else (im, -re)
    if 4 * k == 3 * n:
        return (im, -re) if sign > 0 else (-im, re)
    angle = sign * 2 * math.pi * k / n
    c, s = math.cos(angle), math.sin(angle)
    if 8 * k == n or 8 * k == 3 * n or 8 * k == 5 * n or 8 * k == 7 * n:
        m = abs(c)
        rm, imm = re * m, im * m
        sc, ss = (1 if c > 0 else -1), (1 if s > 0 else -1)
        first = (rm if sc > 0 else -rm) - imm if ss > 0 else (rm if sc > 0 else -rm) + imm
        second = (imm if sc > 0 else -imm) + rm if ss > 0 else (imm if sc > 0 else -imm) - rm
        return first, second
    return re * c - im * s, re * s + im * c


def complex_fft(values, sign):
    n = len(values)
    if n == 1:
        return values
    even = complex_fft(values[0::2], sign)
    odd = complex_fft(values[1::2], sign)
    outs = [None] * n
    for k in range(n // 2):
        re, im = times_root(odd[k][0], odd[k][1], k, n, sign)
        outs[k] = (even[k][0] + re, even[k][1] + im)
        outs[k + n // 2] = (even[k][0] - re, even[k][1] - im)
    return outs


def real_fft(values):
    n = len(values)
    if n == 2:
        return [(values[0] + values[1], None), (values[0] - values[1], None)]
    even, odd = real_fft(values[0::2]), real_fft(values[1::2])
    half = n // 2
    outs = [None] * (half + 1)
    outs[0] = (even[0][0] + odd[0][0], None)
    outs[half] = (even[0][0] - odd[0][0], None)
    for k in range(1, half // 2 + 1):
        if 4 * k == n:
            outs[k] = (even[k][0], -odd[k][0])
            continue
        re, im = times_root(odd[k][0], odd[k][1], k, n, -1)
        outs[k] = (even[k][0] + re, even[k][1] + im)
        outs[half - k] = (even[k][0] - re, im - even[k][1])
    return outs


def real_inverse(values):
    half = len(values) - 1
    n = 2 * half
    if n == 2:
        return [values[0][0] + values[1][0], values[0][0] - values[1][0]]
    even, odd = [None] * (half // 2 + 1), [None] * (half // 2 + 1)
    even[0] = (values[0][0] + values[half][0], None)
    odd[0] = (values[0][0] - values[half][0], None)
    for k in range(1, half // 2 + 1):
        if 4 * k == n:
            even[k] = (values[k][0] * 2.0, None)
            odd[k] = (values[k][1] * -2.0, None)
            continue
        (ar, ai), (br, bi) = values[k], values[half - k]
        even[k] = (ar + br, ai - bi)
        odd[k] = times_root(ar - br, ai + bi, k, n, 1)
    low, high = real_inverse(even), real_inverse(odd)
    outs = [None] * n
    outs[0::2] = low
    outs[1::2] = high
    return outs


def split(values):
    high = values.astype(BF16)
    return high, (values - high.astype(F32)).astype(BF16)


def dot(a, b):
    return jnp.dot(a, b, preferred_element_type=F32)


def table_times(high, low, values):
    vh, vl = split(values)
    return dot(high, vh) + (dot(low, vh) + dot(high, vl))


def times_table(values, high, low):
    vh, vl = split(values)
    return dot(vh, high) + (dot(vh, low) + dot(vl, high))


def loop(count, step):
    lax.fori_loop(0, count, lambda i, c: (step(i), c)[1], 0)


def tile(t):
    return pl.ds(pl.multiple_of(t * 8, 8), 8)


def row_forward(load, mat, scratch, out):
    def first(t):
        spectrum = real_fft(load(t))
        scratch[0, tile(t), :] = spectrum[0][0]
        scratch[0, pl.ds(pl.multiple_of(LANES + t * 8, 8), 8), :] = spectrum[8][0]
        for j in range(1, 8):
            scratch[j, tile(t), :] = spectrum[j][0]
            scratch[j, pl.ds(pl.multiple_of(LANES + t * 8, 8), 8), :] = spectrum[j][1]

    def second(j):
        result = table_times(mat[0, j], mat[1, j], scratch[j])
        out[:, j] = result.reshape(16, 2, 8, LANES)

    loop(16, first)
    loop(8, second)


def row_inverse(load, mat, scratch, emit):
    def first(j):
        scratch[j] = table_times(mat[0, j], mat[1, j], load(j))

    def second(t):
        upper = pl.ds(pl.multiple_of(LANES + t * 8, 8), 8)
        spectrum = [(scratch[0, tile(t), :], None)]
        spectrum += [(scratch[j, tile(t), :], scratch[j, upper, :]) for j in range(1, 8)]
        spectrum.append((scratch[0, upper, :], None))
        emit(t, real_inverse(spectrum))

    loop(8, first)
    loop(16, second)


def col_forward(received, first_mask, mats, twiddle, scratch, emit):
    def transform(values, at):
        spectrum = complex_fft(values, -1)
        for k in range(16):
            re, im = spectrum[k]
            if k:
                c, s = twiddle[k, 0], twiddle[k, 1]
                re, im = re * c + im * s, im * c - re * s
            rows = pl.ds(pl.multiple_of((k % 2) * ROWS_KY + at * 8, 8), 8)
            scratch[k // 2, rows, 0:LANES] = re
            scratch[k // 2, rows, LANES : 2 * LANES] = im

    zero = jnp.zeros((8, LANES), F32)
    transform(
        [(received[b, 0, 0], jnp.where(first_mask, 0.0, received[b, 0, 1])) for b in range(16)], 0
    )
    transform([(jnp.where(first_mask, received[b, 0, 1], 0.0), zero) for b in range(16)], 8)
    loop(7, lambda i: transform([(received[b, i + 1, 0], received[b, i + 1, 1]) for b in range(16)], i + 1))
    loop(8, lambda c: emit(c, times_table(scratch[c], mats[0, 0], mats[0, 1])))


def col_inverse(load, first_mask, mats, twiddle, scratch, out):
    def first(c):
        scratch[c] = times_table(load(c), mats[1, 0], mats[1, 1])

    def transform(at):
        values = []
        for k in range(16):
            rows = pl.ds(pl.multiple_of((k % 2) * ROWS_KY + at * 8, 8), 8)
            re = scratch[k // 2, rows, 0:LANES]
            im = scratch[k // 2, rows, LANES : 2 * LANES]
            if k:
                c, s = twiddle[k, 0], twiddle[k, 1]
                re, im = re * c - im * s, im * c + re * s
            values.append((re, im))
        return complex_fft(values, 1)

    def second(j):
        for b, (re, im) in enumerate(transform(j)):
            out[b, j, 0] = re
            out[b, j, 1] = im

    loop(8, first)
    extra = transform(8)
    for b in range(16):
        out[b, 0, 0] = extra[b][0]
    for b, (re, im) in enumerate(transform(0)):
        out[b, 0, 1] = jnp.where(first_mask, out[b, 0, 0], im)
        out[b, 0, 0] = re
    loop(7, lambda i: second(i + 1))


def bit(value, k):
    return (value // (1 << k)) % 2


def partner(me, i):
    core = me % 2
    offset = i * (1 - core) + (16 - i) * core
    return sum(((bit(me, k) + bit(offset, k)) % 2) * (1 << k) for k in range(4))


def kernel(
    vort, row_hbm, col_mats, twiddle, flips, ky_ref,
    grad, resid,
    rowm, grid_a, grid_u, grid_v, grid_wx, grid_wy, sends, recvs, local_b,
    row_s, col_s, w_spec, e_spec, adj, next_start, prev_end,
    dx_t, linv_t, decay_t, nlf_t, flat,
    table_sem, own_sem, send_sem, recv_sem, seg_send, seg_recv,
):
    me = lax.axis_index("space")
    seg = lax.axis_index("seg")
    after, before = (seg + 1) % 8, (seg + 7) % 8
    rows_in_tile = lax.broadcasted_iota(jnp.int32, (8, LANES), 0)
    first_mask = (rows_in_tile == 0) & (jnp.zeros((8, LANES), jnp.int32) + me == 0)

    def table_copy(i):
        return pltpu.make_async_copy(row_hbm.at[i], rowm.at[i], table_sem.at[i])

    for i in (0, 3, 2, 1):
        table_copy(i).start()

    barrier = pltpu.get_barrier_semaphore()
    loop(15, lambda i: pl.semaphore_signal(
        barrier, inc=1, device_id={"space": partner(me, i + 1)}, device_id_type=MESH))
    for s in (after, before):
        pl.semaphore_signal(barrier, inc=1, device_id={"seg": s}, device_id_type=MESH)

    def copy_to(f, i):
        p = partner(me, i)
        return pltpu.make_async_remote_copy(
            src_ref=sends.at[f, p], dst_ref=recvs.at[f, me],
            send_sem=send_sem.at[f, i - 1], recv_sem=recv_sem.at[f, i - 1],
            device_id={"space": p}, device_id_type=MESH)

    def own_copy(f):
        return pltpu.make_async_copy(sends.at[f, me], recvs.at[f, me], own_sem.at[f])

    def start(f):
        own_copy(f).start()
        loop(15, lambda i: copy_to(f, i + 1).start())

    def finish(f):
        own_copy(f).wait()

        def one(i):
            copy = copy_to(f, i + 1)
            copy.wait_recv()
            copy.wait_send()

        loop(15, one)

    def seg_copy(i):
        source, target, s = ((w_spec, next_start, before), (e_spec, prev_end, after))[i]
        return pltpu.make_async_remote_copy(
            src_ref=source, dst_ref=target, send_sem=seg_send.at[i], recv_sem=seg_recv.at[i],
            device_id={"seg": s}, device_id_type=MESH)

    for b in range(16):
        grid_a[b] = vort[:, b * LANES : (b + 1) * LANES].T
    table_copy(0).wait()
    row_forward(lambda t: [grid_a[b, tile(t), :] for b in range(16)], rowm.at[0], row_s, sends.at[0])
    pl.semaphore_wait(barrier, 17)
    start(0)

    def stacked(f):
        return lambda j: sends[f, :, j].reshape(256, LANES)

    def arrived(f):
        return lambda j: recvs[f, :, j].reshape(256, LANES)

    def keep(ref):
        def emit(t, tiles):
            for b in range(16):
                ref[b, tile(t), :] = tiles[b]
        return emit

    table_copy(3).wait()
    row_inverse(stacked(0), rowm.at[3], row_s, keep(grid_wy))

    flat[...] = jnp.zeros_like(flat)

    def make_tables(c):
        rows = lax.broadcasted_iota(jnp.int32, (PAIR, LANES), 0)
        lanes = lax.broadcasted_iota(jnp.int32, (PAIR, LANES), 1)
        k = 2 * c + jnp.where(rows >= ROWS_KY, 1, 0) + 16 * lanes
        kx = jnp.where(k < N // 2, k, k - N)
        ky = ky_ref[...]
        kxf = kx.astype(F32)
        square = kxf * kxf + ky * ky
        decay = jnp.exp(-TIME_STEP * (DRAG + 9.0 * square / (N * N)))
        dx_t[c] = jnp.where(kx == -(N // 2), 0.0, kxf)
        linv_t[c] = jnp.where(square > 0.0, 1.0 / jnp.maximum(square, 1.0), 0.0)
        decay_t[c] = decay
        inside = (3.0 * jnp.abs(kxf) <= N) & (3.0 * jnp.abs(ky) <= N)
        nlf_t[c] = jnp.where(inside, TIME_STEP * decay, 0.0)

    loop(8, make_tables)

    finish(0)

    def put_w(c, value):
        w_spec[c] = value

    col_forward(recvs.at[0], first_mask, col_mats, twiddle, col_s, put_w)
    seg_copy(0).start()

    def two(re, im):
        return jnp.concatenate([re, im], axis=1)

    def halves(ref, c):
        return ref[c, :, 0:LANES], ref[c, :, LANES : 2 * LANES]

    def psi_hat(c):
        re, im = halves(w_spec, c)
        linv = linv_t[c]
        return two(linv * re, linv * im)

    def v_hat(c):
        re, im = halves(w_spec, c)
        factor = linv_t[c] * dx_t[c]
        return two(factor * im, -factor * re)

    def wx_hat(c):
        re, im = halves(w_spec, c)
        factor = dx_t[c]
        return two(-factor * im, factor * re)

    for f, hat in ((1, psi_hat), (2, v_hat), (3, wx_hat)):
        col_inverse(hat, first_mask, col_mats, twiddle, col_s, sends.at[f])
        start(f)

    finish(1)
    row_inverse(arrived(1), rowm.at[3], row_s, keep(grid_u))
    table_copy(2).wait()
    finish(2)
    row_inverse(arrived(2), rowm.at[2], row_s, keep(grid_v))
    finish(3)

    def nonlinear(t, tiles):
        for b in range(16):
            grid_wx[b, tile(t), :] = tiles[b]
            grid_a[b, tile(t), :] = (
                grid_u[b, tile(t), :] * tiles[b] + grid_v[b, tile(t), :] * grid_wy[b, tile(t), :]
            )

    row_inverse(arrived(3), rowm.at[2], row_s, nonlinear)
    row_forward(lambda t: [grid_a[b, tile(t), :] for b in range(16)], rowm.at[0], row_s, sends.at[4])
    start(4)
    table_copy(1).wait()
    seg_copy(0).wait_recv()
    finish(4)

    def put_end(c, value):
        re, im = halves(w_spec, c)
        decay, nlf, dx = decay_t[c], nlf_t[c], dx_t[c]
        forced = (dx == 0.0) & (nlf > 0.0) & (ky_ref[...] == float(FORCING_WAVE))
        force = jnp.where(forced, TIME_STEP * FORCE_AMP * (N * N / 2.0) * decay, 0.0)
        end_re = decay * re - nlf * value[:, 0:LANES] + force
        end_im = decay * im - nlf * value[:, LANES : 2 * LANES]
        e_spec[c] = two(end_re, end_im)
        next_re, next_im = halves(next_start, c)
        adj[c] = two(end_re - next_re, end_im - next_im)

    col_forward(recvs.at[4], first_mask, col_mats, twiddle, col_s, put_end)

    def weight_hat(c):
        re, im = halves(adj, c)
        nlf = nlf_t[c]
        return two(nlf * re, nlf * im)

    col_inverse(weight_hat, first_mask, col_mats, twiddle, col_s, sends.at[5])
    start(5)
    seg_copy(1).start()
    finish(5)
    row_inverse(arrived(5), rowm.at[2], row_s, keep(grid_a))

    def product(ref):
        return lambda t: [grid_a[b, tile(t), :] * ref[b, tile(t), :] for b in range(16)]

    row_forward(product(grid_u), rowm.at[0], row_s, sends.at[6])
    start(6)
    row_forward(product(grid_wx), rowm.at[1], row_s, sends.at[7])
    start(7)
    row_forward(product(grid_wy), rowm.at[0], row_s, sends.at[8])
    start(8)
    row_forward(product(grid_v), rowm.at[1], row_s, local_b)

    seg_copy(1).wait_recv()
    seg_copy(1).wait_send()
    seg_copy(0).wait_send()

    def make_residual(c):
        prev_re, prev_im = halves(prev_end, c)
        re, im = halves(w_spec, c)
        res_re, res_im = prev_re - re, prev_im - im
        prev_end[c] = two(res_re, res_im)
        adj_re, adj_im = halves(adj, c)
        decay = decay_t[c]
        adj[c] = two(decay * adj_re - res_re, decay * adj_im - res_im)

    loop(8, make_residual)

    slots = slot_table()

    def write_residual(k, mirror, flip):
        for part in range(2):
            lanes = slice(part * LANES, (part + 1) * LANES)
            for j in range(8):
                rows = pl.ds(pl.multiple_of((k % 2) * ROWS_KY + j * 8, 8), 8)
                direct = prev_end[k // 2, rows, lanes]
                rows = pl.ds(pl.multiple_of((mirror % 2) * ROWS_KY + j * 8, 8), 8)
                mirrored = prev_end[mirror // 2, rows, lanes]
                if part:
                    mirrored = -mirrored
                for h in range(2):
                    to = int(slots[j, 4 * h])
                    flat[part, 0, pl.ds(to, 4, stride=16), :] = direct[4 * h : 4 * h + 4]
                    flat[part, 1, pl.ds(64 + to, 4, stride=16), :] = mirrored[4 * h : 4 * h + 4]
            rows = pl.ds(pl.multiple_of((k % 2) * ROWS_KY + 64, 8), 8)
            extra = prev_end[k // 2, rows, lanes]
            flat[part, 0, 64:72, :] = jnp.where(first_mask, extra, 0.0)
            flat[part, 1, 64:72, :] = jnp.where(first_mask, 0.0, flat[part, 1, 64:72, :])
            high, low = split(jnp.concatenate([flat[part, 0], flat[part, 1]], axis=1))
            contract = (((1,), (1,)), ((), ()))
            result = lax.dot_general(flip, high, contract, preferred_element_type=F32)
            result = result + lax.dot_general(flip, low, contract, preferred_element_type=F32)
            resid[part, :, k, :] = result

    write_residual(0, 0, flips[0])
    loop(15, lambda i: write_residual(i + 1, 15 - i, flips[1]))

    finish(6)

    def add_a(c, value):
        re, im = halves(adj, c)
        dx = dx_t[c]
        adj[c] = two(re - dx * value[:, LANES : 2 * LANES], im + dx * value[:, 0:LANES])

    col_forward(recvs.at[6], first_mask, col_mats, twiddle, col_s, add_a)
    finish(7)

    def add_c(c, value):
        re, im = halves(adj, c)
        linv = linv_t[c]
        adj[c] = two(re + linv * value[:, 0:LANES], im + linv * value[:, LANES : 2 * LANES])

    col_forward(recvs.at[7], first_mask, col_mats, twiddle, col_s, add_c)
    finish(8)

    def add_d(c, value):
        re, im = halves(adj, c)
        factor = linv_t[c] * dx_t[c]
        adj[c] = two(re + factor * value[:, LANES : 2 * LANES], im - factor * value[:, 0:LANES])

    col_forward(recvs.at[8], first_mask, col_mats, twiddle, col_s, add_d)
    col_inverse(lambda c: adj[c], first_mask, col_mats, twiddle, col_s, sends.at[9])
    start(9)
    finish(9)

    def total(j):
        return (recvs[9, :, j] + local_b[:, j]).reshape(256, LANES)

    row_inverse(total, rowm.at[2], row_s, keep(grid_a))
    for b in range(16):
        grad[:, b * LANES : (b + 1) * LANES] = grid_a[b].T


def body(vorticity):
    device = lax.axis_index("space")
    col_mats, twiddle = col_tables()
    waves = slot_table().reshape(64, 1).astype(np.float32)
    ky = jnp.asarray(waves) + 64.0 * device.astype(F32)
    ky = jnp.concatenate([ky, jnp.full((8, 1), N // 2, F32)], axis=0)
    ky = jnp.broadcast_to(jnp.concatenate([ky, ky], axis=0), (PAIR, LANES))
    vmem = pl.BlockSpec(memory_space=pltpu.VMEM)
    slab = (16, 8, 2, 8, LANES)
    grid = pltpu.VMEM((16, LANES, LANES), F32)
    spectrum = pltpu.VMEM((8, PAIR, 2 * LANES), F32)
    factor = pltpu.VMEM((8, PAIR, LANES), F32)
    gradient, residual = pl.pallas_call(
        kernel,
        out_shape=(
            jax.ShapeDtypeStruct((LANES, N), F32),
            jax.ShapeDtypeStruct((2, LANES, 16, LANES), F32),
        ),
        in_specs=[vmem, pl.BlockSpec(memory_space=pl.ANY), vmem, vmem, vmem, vmem],
        out_specs=(vmem, vmem),
        scratch_shapes=[
            pltpu.VMEM((4, 2, 8, 256, 256), BF16),
            grid, grid, grid, grid, grid,
            pltpu.VMEM((10,) + slab, F32),
            pltpu.VMEM((10,) + slab, F32),
            pltpu.VMEM(slab, F32),
            pltpu.VMEM((8, 256, LANES), F32),
            spectrum, spectrum, spectrum, spectrum, spectrum, spectrum,
            factor, factor, factor, factor,
            pltpu.VMEM((2, 2, LANES, LANES), F32),
            pltpu.SemaphoreType.DMA((4,)),
            pltpu.SemaphoreType.DMA((10,)),
            pltpu.SemaphoreType.DMA((10, 15)),
            pltpu.SemaphoreType.DMA((10, 15)),
            pltpu.SemaphoreType.DMA((2,)),
            pltpu.SemaphoreType.DMA((2,)),
        ],
        compiler_params=pltpu.CompilerParams(
            collective_id=0, has_side_effects=True, vmem_limit_bytes=60 * 2**20
        ),
        name="orbit_gradient",
    )(vorticity[0], jnp.asarray(row_tables()), jnp.asarray(col_mats), jnp.asarray(twiddle),
      jnp.asarray(flip_tables()), ky)
    return gradient[None], residual.reshape(1, 2, N, LANES)


def solution(mesh):
    return jax.shard_map(
        body,
        mesh=mesh,
        in_specs=(P("seg", "space", None),),
        out_specs=(P("seg", "space", None), P("seg", None, None, "space")),
        check_vma=False,
    )
```

time: 719 us -> 227 us (0.32)
  the two profiles are of different devices: /device:TPU:1 before, /device:TPU:33 now
where the time goes in v1:
time: 227 us
  Pallas kernels  221 us (97%)
  local copies, waits for them, and re-layouts  4.49 us (2%)
    pallas_call x1, Pallas kernels, body(): pl.pallas_call(kernel, out_shape=(jax.ShapeDtypeStruct((LANES, N), F32),...  221 us

profile of v1, /device:TPU:33, one launch (start us, length us, event | category | flops | bytes accessed | tf_op | source)
XLA Modules:
  0.0 226.6 jit_solution(13339557688668603805)
XLA Ops:
  0.6 0.7 broadcast_add_fusion
  1.3 0.1 pad_maximum_fusion
  1.4 0.7 broadcast_in_dim.11.ky_ref
  2.1 220.7 %orbit_gradient.1 = (f32[128,2048]{1,0:T(8,128)}, f32[2,128,16,128]{3,2,1,0:T(8,128)}) custom-call(f32[128,2048]{1,0:T(8,128)} %bitcast.5, bf16[4,2,8,256,256]{4,3,2,1,0:T(8,128)(2,1)} %constant.19.clone.row_hbm, bf16[2,2,256,256]{3,2,1,0:T(8,128)(2,1)} %constant.20.clone.col_mats, f32[16,2,8,128]{3,2,1,0:T(8,128)} %constant.21.clone.twiddle, ...), custom_call_target="tpu_custom_call" | custom-call | tf_op jit(solution)/shard_map/orbit_gradient/pallas_call | solution.py:596
  222.8 0.0 copy-start
  222.9 2.4 %copy.10 = f32[1,128,2048]{2,1,0:T(8,128)} copy(f32[1,128,2048]{2,1,0:T(8,128)} %bitcast.6) | data formatting | bytes 2097152
  225.3 0.0 copy-done
  225.3 1.3 copy.11
  (1 shorter events, 0.0 us)
Async XLA Ops:
  222.8 2.5 %copy-start = (f32[2,128,16,128]{3,2,1,0:T(8,128)S(1)}, f32[2,128,16,128]{3,2,1,0:T(8,128)}, u32[]{:S(2)}) copy-start(f32[2,128,16,128]{3,2,1,0:T(8,128)} %get-tuple-element.5) | copy-start | bytes 6291460

commit v2 on v1

v2 whole, which is shorter than its diff:
```python
import functools
import math

import jax
import jax.numpy as jnp
import ml_dtypes
import numpy as np
from jax import lax
from jax.experimental import pallas as pl
from jax.experimental.pallas import tpu as pltpu
from jax.sharding import PartitionSpec as P

N = 2048
SLABS = 16
LANES = 128
GROUPS = ((0, 8, 1, 2, 3), (4, 5, 6, 7))
GROUP_J = (0, 4)
ROWS_OF = (40, 32)
FIRST_ROW = (0, 640)
CHUNK = (160, 128)
ALL_ROWS = 16 * (40 + 32)
KEPT = 11
TIME_STEP = 0.3
DRAG = 0.05
FORCE_AMP = 0.8
FORCING_WAVE = 4
MESH = pl.DeviceIdType.MESH
F32 = jnp.float32
BF16 = jnp.bfloat16


def split_table(table):
    high = table.astype(np.float32).astype(ml_dtypes.bfloat16)
    low = (table - high.astype(np.float64)).astype(np.float32).astype(ml_dtypes.bfloat16)
    return high, low


def slot_wave(j, d, r):
    if r < 4:
        return j + 16 * (4 * d + r)
    return (16 - j if j else 8) + 16 * (4 * d + r - 4)


@functools.cache
def row_tables():
    a = np.arange(LANES)
    forward = np.zeros((8, 16, 2, 8, 2, LANES))
    inverse = np.zeros((8, 2, LANES, 16, 2, 8))
    wave = np.zeros((8, 16, 8))
    for j in range(8):
        for d in range(16):
            for r in range(8):
                k = slot_wave(j, d, r)
                wave[j, d, r] = k
                c = np.cos(2 * np.pi * ((a * k) % N) / N)
                s = np.sin(2 * np.pi * ((a * k) % N) / N)
                if j == 0:
                    part = 0 if r < 4 else 1
                    forward[j, d, 0, r, part] = c
                    forward[j, d, 1, r, part] = -s
                    inverse[j, part, :, d, 0, r] = 2 * c
                    inverse[j, part, :, d, 1, r] = -2 * s
                    if k == 0:
                        alternate = 1.0 - 2.0 * (a % 2)
                        forward[j, d, 1, r, part] = alternate
                        inverse[j, part, :, d, 0, r] = 1.0
                        inverse[j, part, :, d, 1, r] = alternate
                else:
                    sign = 1.0 if r < 4 else -1.0
                    forward[j, d, 0, r, 0] = c
                    forward[j, d, 0, r, 1] = sign * s
                    forward[j, d, 1, r, 0] = -s
                    forward[j, d, 1, r, 1] = sign * c
                    inverse[j, 0, :, d, 0, r] = c
                    inverse[j, 0, :, d, 1, r] = -s
                    inverse[j, 1, :, d, 0, r] = sign * s
                    inverse[j, 1, :, d, 1, r] = sign * c
    inverse /= N
    dwave = wave[:, :, None, :, None, None]
    forward_dy = np.stack([-forward[:, :, 1], forward[:, :, 0]], axis=2) * dwave
    inverse_dy = np.stack([inverse[..., 1, :], -inverse[..., 0, :]], axis=-2) * wave[:, None, None, :, None, :]
    shape = (8, 256, 256)
    outs = []
    for table in (forward, forward_dy, inverse, inverse_dy):
        high, low = split_table(table.reshape(shape))
        outs.append(np.stack([high, low]))
    return np.stack(outs)


@functools.cache
def col_tables():
    a = np.arange(LANES)
    angle = 2 * np.pi * (np.outer(a, a) % LANES) / LANES
    c, s = np.cos(angle), np.sin(angle)
    forward = np.block([[c, -s], [s, c]])
    inverse = np.block([[c, s], [-s, c]]) / N
    mats = np.stack([np.stack(split_table(m)) for m in (forward, inverse)])
    angle = 2 * np.pi * np.outer(np.arange(16), a) / N
    twiddle = np.stack([np.cos(angle), np.sin(angle)], axis=1)
    twiddle = np.broadcast_to(twiddle[:, :, None, :], (16, 2, 8, LANES)).astype(np.float32)
    return mats, np.ascontiguousarray(twiddle)


@functools.cache
def flip_tables():
    eye = np.eye(LANES)
    first = np.concatenate([eye, eye[(LANES - np.arange(LANES)) % LANES]], axis=1)
    other = np.concatenate([eye, eye[LANES - 1 - np.arange(LANES)]], axis=1)
    return (np.stack([first, other]) / N).astype(ml_dtypes.bfloat16)


@functools.cache
def slot_table():
    return np.array([[slot_wave(j, 0, r) for r in range(8)] for j in range(8)], np.int32)


@functools.cache
def wave_table():
    table = np.zeros((2, CHUNK[0] + CHUNK[1], LANES), np.float32)
    row = 0
    for group in GROUPS:
        for _ in range(4):
            for j in group:
                table[0, row : row + 8] = (N // 2) if j == 8 else slot_table()[j][:, None]
                table[1, row : row + 8] = 0 if j == 8 else 64
                row += 8
    return table


def times_root(re, im, k, n, sign):
    k = k % n
    if im is None:
        if k == 0:
            return re, None
        angle = sign * 2 * math.pi * k / n
        if 4 * k == n:
            return None, (re if sign > 0 else -re)
        return re * math.cos(angle), re * math.sin(angle)
    if k == 0:
        return re, im
    if 2 * k == n:
        return -re, -im
    if 4 * k == n:
        return (-im, re) if sign > 0 else (im, -re)
    if 4 * k == 3 * n:
        return (im, -re) if sign > 0 else (-im, re)
    angle = sign * 2 * math.pi * k / n
    c, s = math.cos(angle), math.sin(angle)
    if 8 * k == n or 8 * k == 3 * n or 8 * k == 5 * n or 8 * k == 7 * n:
        m = abs(c)
        rm, imm = re * m, im * m
        sc, ss = (1 if c > 0 else -1), (1 if s > 0 else -1)
        first = (rm if sc > 0 else -rm) - imm if ss > 0 else (rm if sc > 0 else -rm) + imm
        second = (imm if sc > 0 else -imm) + rm if ss > 0 else (imm if sc > 0 else -imm) - rm
        return first, second
    return re * c - im * s, re * s + im * c


def complex_fft(values, sign):
    n = len(values)
    if n == 1:
        return values
    even = complex_fft(values[0::2], sign)
    odd = complex_fft(values[1::2], sign)
    outs = [None] * n
    for k in range(n // 2):
        re, im = times_root(odd[k][0], odd[k][1], k, n, sign)
        outs[k] = (even[k][0] + re, even[k][1] + im)
        outs[k + n // 2] = (even[k][0] - re, even[k][1] - im)
    return outs


def real_fft(values):
    n = len(values)
    if n == 2:
        return [(values[0] + values[1], None), (values[0] - values[1], None)]
    even, odd = real_fft(values[0::2]), real_fft(values[1::2])
    half = n // 2
    outs = [None] * (half + 1)
    outs[0] = (even[0][0] + odd[0][0], None)
    outs[half] = (even[0][0] - odd[0][0], None)
    for k in range(1, half // 2 + 1):
        if 4 * k == n:
            outs[k] = (even[k][0], -odd[k][0])
            continue
        re, im = times_root(odd[k][0], odd[k][1], k, n, -1)
        outs[k] = (even[k][0] + re, even[k][1] + im)
        outs[half - k] = (even[k][0] - re, im - even[k][1])
    return outs


def real_inverse(values):
    half = len(values) - 1
    n = 2 * half
    if n == 2:
        return [values[0][0] + values[1][0], values[0][0] - values[1][0]]
    even, odd = [None] * (half // 2 + 1), [None] * (half // 2 + 1)
    even[0] = (values[0][0] + values[half][0], None)
    odd[0] = (values[0][0] - values[half][0], None)
    for k in range(1, half // 2 + 1):
        if 4 * k == n:
            even[k] = (values[k][0] * 2.0, None)
            odd[k] = (values[k][1] * -2.0, None)
            continue
        (ar, ai), (br, bi) = values[k], values[half - k]
        even[k] = (ar + br, ai - bi)
        odd[k] = times_root(ar - br, ai + bi, k, n, 1)
    low, high = real_inverse(even), real_inverse(odd)
    outs = [None] * n
    outs[0::2] = low
    outs[1::2] = high
    return outs


def split(values):
    high = values.astype(BF16)
    return high, (values - high.astype(F32)).astype(BF16)


def dot(a, b):
    return jnp.dot(a, b, preferred_element_type=F32)


def table_times(high, low, values):
    vh, vl = split(values)
    return dot(high, vh) + (dot(low, vh) + dot(high, vl))


def times_table(values, high, low):
    vh, vl = split(values)
    return dot(vh, high) + (dot(vh, low) + dot(vl, high))


def loop(count, step, unroll=4):
    lax.fori_loop(0, count, lambda i, c: (step(i), c)[1], 0, unroll=unroll)


def tile(t, base=0):
    return pl.ds(pl.multiple_of(base + t * 8, 8), 8)


def chunk(g, c):
    return pl.ds(pl.multiple_of(FIRST_ROW[g] + c * CHUNK[g], 8), CHUNK[g])


def tile_rows(k, j):
    g = 0 if j in GROUPS[0] else 1
    start = FIRST_ROW[g] + GROUPS[g].index(j) * 8
    if isinstance(k, int):
        return pl.ds(start + k * ROWS_OF[g], 8)
    return pl.ds(pl.multiple_of(start + k * ROWS_OF[g], 8), 8)


def row_short_forward(t, tiles, scratch):
    spectrum = real_fft(tiles)
    scratch[0, tile(t), :] = spectrum[0][0]
    scratch[0, tile(t, LANES), :] = spectrum[8][0]
    for j in range(1, 8):
        scratch[j, tile(t), :] = spectrum[j][0]
        scratch[j, tile(t, LANES), :] = spectrum[j][1]


def row_long_forward(g, mat, scratch, out):
    def step(i):
        j = i + GROUP_J[g]
        result = table_times(mat[0, j], mat[1, j], scratch[j])
        out[:, j] = result.reshape(16, 2, 8, LANES)

    loop(4, step)


def row_long_inverse(g, load, mat, scratch):
    def step(i):
        j = i + GROUP_J[g]
        scratch[j] = table_times(mat[0, j], mat[1, j], load(j))

    loop(4, step)


def row_short_inverse(t, scratch):
    spectrum = [(scratch[0, tile(t), :], None)]
    spectrum += [(scratch[j, tile(t), :], scratch[j, tile(t, LANES), :]) for j in range(1, 8)]
    spectrum.append((scratch[0, tile(t, LANES), :], None))
    return real_inverse(spectrum)


def col_forward(g, received, first_mask, mats, twiddle, scratch, emit):
    def transform(values, start):
        spectrum = complex_fft(values, -1)
        for k in range(16):
            re, im = spectrum[k]
            if k:
                c, s = twiddle[k, 0], twiddle[k, 1]
                re, im = re * c + im * s, im * c - re * s
            rows = pl.ds(start + k * ROWS_OF[g], 8)
            scratch[rows, 0:LANES] = re
            scratch[rows, LANES : 2 * LANES] = im

    for n, j in enumerate(GROUPS[g]):
        start = FIRST_ROW[g] + n * 8
        if j == 0:
            values = [
                (received[b, 0, 0], jnp.where(first_mask, 0.0, received[b, 0, 1])) for b in range(16)
            ]
        elif j == 8:
            zero = jnp.zeros((8, LANES), F32)
            values = [(jnp.where(first_mask, received[b, 0, 1], 0.0), zero) for b in range(16)]
        else:
            values = [(received[b, j, 0], received[b, j, 1]) for b in range(16)]
        transform(values, start)

    def step(c):
        rows = chunk(g, c)
        emit(rows, c, times_table(scratch[rows, :], mats[0, 0], mats[0, 1]))

    loop(4, step)


def col_inverse(g, load, first_mask, mats, twiddle, scratch, out):
    def step(c):
        rows = chunk(g, c)
        scratch[rows, :] = times_table(load(rows), mats[1, 0], mats[1, 1])

    loop(4, step)

    def transform(n):
        values = []
        for k in range(16):
            rows = pl.ds(FIRST_ROW[g] + n * 8 + k * ROWS_OF[g], 8)
            re = scratch[rows, 0:LANES]
            im = scratch[rows, LANES : 2 * LANES]
            if k:
                c, s = twiddle[k, 0], twiddle[k, 1]
                re, im = re * c - im * s, im * c + re * s
            values.append((re, im))
        return complex_fft(values, 1)

    if g == 0:
        for b, (re, im) in enumerate(transform(1)):
            out[b, 0, 0] = re
        for b, (re, im) in enumerate(transform(0)):
            out[b, 0, 1] = jnp.where(first_mask, out[b, 0, 0], im)
            out[b, 0, 0] = re
    for n, j in enumerate(GROUPS[g]):
        if j not in (0, 8):
            for b, (re, im) in enumerate(transform(n)):
                out[b, j, 0] = re
                out[b, j, 1] = im


def partners(me):
    core = me % 2
    step = [(1 - 2 * ((me // (1 << k)) % 2)) * (1 << k) for k in range(4)]

    def other(offset):
        return me + sum(step[k] for k in range(4) if (offset >> k) & 1)

    return [other(i) * (1 - core) + other(16 - i) * core for i in range(1, 16)]


def kernel(
    vort, row_hbm, col_mats, twiddle, flips, waves,
    grad, resid,
    rowm, grid_a, grid_u, grid_v, grid_wx, grid_wy, sends, recvs, local_b,
    row_s, col_s, w_spec, e_spec, adj, next_start, prev_end,
    dx_t, linv_t, decay_t, nlf_t, flat, grad_v, resid_v,
    table_sem, out_sem, own_sem, send_sem, recv_sem, seg_send, seg_recv,
):
    me = lax.axis_index("space")
    seg = lax.axis_index("seg")
    after, before = (seg + 1) % 8, (seg + 7) % 8
    rows_in_tile = lax.broadcasted_iota(jnp.int32, (8, LANES), 0)
    first_mask = (rows_in_tile == 0) & (jnp.zeros((8, LANES), jnp.int32) + me == 0)
    others = partners(me)
    both = (0, 1)

    def table_copy(i):
        return pltpu.make_async_copy(row_hbm.at[i], rowm.at[i], table_sem.at[i])

    for i in (0, 3, 2, 1):
        table_copy(i).start()

    barrier = pltpu.get_barrier_semaphore()
    for p in others:
        pl.semaphore_signal(barrier, inc=1, device_id={"space": p}, device_id_type=MESH)
    for s in (after, before):
        for p in others + [me]:
            pl.semaphore_signal(
                barrier, inc=1, device_id={"seg": s, "space": p}, device_id_type=MESH)

    def part(f, g, p):
        return (f, p, pl.ds(GROUP_J[g], 4))

    def own_copy(f, g):
        return pltpu.make_async_copy(
            sends.at[part(f, g, me)], recvs.at[part(f, g, me)], own_sem.at[f, g])

    def start(f, g):
        own_copy(f, g).start()

        def one(p):
            pltpu.make_async_remote_copy(
                src_ref=sends.at[part(f, g, p)], dst_ref=recvs.at[part(f, g, me)],
                send_sem=send_sem.at[f, g], recv_sem=recv_sem.at[f, g],
                device_id={"space": p}, device_id_type=MESH).start()

        if f == 4:
            for p in others:
                pl.when(p < KEPT)(functools.partial(one, p))
        elif f == 5:
            @pl.when(me < KEPT)
            def _():
                for p in others:
                    one(p)
        else:
            for p in others:
                one(p)

    def wait_bytes(f, g, sem, count):
        pltpu.make_async_copy(
            sends.at[part(f, g, pl.ds(0, count))], recvs.at[part(f, g, pl.ds(0, count))],
            sem.at[f, g]).wait()

    def some(f, g, sem):
        @pl.when(me < KEPT)
        def _():
            wait_bytes(f, g, sem, KEPT - 1)

        @pl.when(me >= KEPT)
        def _():
            wait_bytes(f, g, sem, KEPT)

    def inside(f, g, sem):
        @pl.when(me < KEPT)
        def _():
            wait_bytes(f, g, sem, 15)

    def finish(f, g):
        own_copy(f, g).wait()
        kind = {4: inside, 5: some}.get(f)
        if kind:
            kind(f, g, recv_sem)
        else:
            wait_bytes(f, g, recv_sem, 15)

    def finish_send(f, g):
        kind = {4: some, 5: inside}.get(f)
        if kind:
            kind(f, g, send_sem)
        else:
            wait_bytes(f, g, send_sem, 15)

    def start_before():
        for p in [me] + others:
            pltpu.make_async_remote_copy(
                src_ref=sends.at[0, p], dst_ref=recvs.at[10, me],
                send_sem=send_sem.at[10, 0], recv_sem=recv_sem.at[10, 0],
                device_id={"seg": before, "space": p}, device_id_type=MESH).start()

    def wait_before(sem):
        pltpu.make_async_copy(sends.at[0], recvs.at[10], sem.at[10, 0]).wait()

    def seg_copy():
        return pltpu.make_async_remote_copy(
            src_ref=e_spec, dst_ref=prev_end, send_sem=seg_send, recv_sem=seg_recv,
            device_id={"seg": after}, device_id_type=MESH)

    for b in range(16):
        grid_a[b] = vort[:, b * LANES : (b + 1) * LANES].T

    def tiles_of(ref, t):
        return [ref[b, tile(t), :] for b in range(16)]

    def keep(ref, t, tiles):
        for b in range(16):
            ref[b, tile(t), :] = tiles[b]

    loop(16, lambda t: row_short_forward(t, tiles_of(grid_a, t), row_s.at[0]))
    table_copy(0).wait()
    for g in both:
        row_long_forward(g, rowm.at[0], row_s.at[0], sends.at[0])
        if g == 0:
            pl.semaphore_wait(barrier, 47)
        start(0, g)

    def stacked(f):
        return lambda j: sends[f, :, j].reshape(256, LANES)

    def arrived(f):
        return lambda j: recvs[f, :, j].reshape(256, LANES)

    for g in both:
        first = 0 if g == 0 else CHUNK[0]
        ky = waves[0, first : first + CHUNK[g], :] + waves[1, first : first + CHUNK[g], :] * me.astype(F32)

        def make_tables(c, g=g, ky=ky):
            rows = lax.broadcasted_iota(jnp.int32, (CHUNK[g], LANES), 0)
            lanes = lax.broadcasted_iota(jnp.int32, (CHUNK[g], LANES), 1)
            k = 4 * c + 16 * lanes
            for q in range(1, 4):
                k = k + jnp.where(rows >= q * ROWS_OF[g], 1, 0)
            kx = jnp.where(k < N // 2, k, k - N)
            kxf = kx.astype(F32)
            square = kxf * kxf + ky * ky
            decay = jnp.exp(-TIME_STEP * (DRAG + 9.0 * square / (N * N)))
            to = chunk(g, c)
            dx_t[to, :] = jnp.where(kx == -(N // 2), 0.0, kxf)
            linv_t[to, :] = jnp.where(square > 0.0, 1.0 / jnp.maximum(square, 1.0), 0.0)
            decay_t[to, :] = decay
            keep_mask = (3.0 * jnp.abs(kxf) <= N) & (3.0 * jnp.abs(ky) <= N)
            nlf_t[to, :] = jnp.where(keep_mask, TIME_STEP * decay, 0.0)

        loop(4, make_tables, 1)

    def zero_columns(b):
        recvs[5, b] = jnp.zeros((8, 2, 8, LANES), F32)

    @pl.when(me >= KEPT)
    def _():
        loop(16, lambda b: recvs.__setitem__((4, b), jnp.zeros((8, 2, 8, LANES), F32)), 1)

    loop(16 - KEPT, lambda b: zero_columns(b + KEPT), 1)
    flat[...] = jnp.zeros_like(flat)

    def two(re, im):
        return jnp.concatenate([re, im], axis=1)

    def halves(ref, rows):
        return ref[rows, 0:LANES], ref[rows, LANES : 2 * LANES]

    def psi_hat(rows):
        re, im = halves(w_spec, rows)
        linv = linv_t[rows, :]
        return two(linv * re, linv * im)

    def v_hat(rows):
        re, im = halves(w_spec, rows)
        factor = linv_t[rows, :] * dx_t[rows, :]
        return two(factor * im, -factor * re)

    def wx_hat(rows):
        re, im = halves(w_spec, rows)
        factor = dx_t[rows, :]
        return two(-factor * im, factor * re)

    def forward_columns(g, f, emit):
        col_forward(g, recvs.at[f], first_mask, col_mats, twiddle, col_s, emit)

    def inverse_columns(g, f, load):
        col_inverse(g, load, first_mask, col_mats, twiddle, col_s, sends.at[f])
        start(f, g)

    def put(ref):
        def emit(rows, c, value):
            ref[rows, :] = value
        return emit

    for g in both:
        finish(0, g)
        forward_columns(g, 0, put(w_spec))
        inverse_columns(g, 1, psi_hat)
        inverse_columns(g, 2, v_hat)
        inverse_columns(g, 3, wx_hat)
    start_before()

    table_copy(3).wait()
    for g in both:
        row_long_inverse(g, stacked(0), rowm.at[3], row_s.at[0])
    loop(16, lambda t: keep(grid_wy, t, row_short_inverse(t, row_s.at[0])))
    table_copy(2).wait()

    for g in both:
        finish(1, g)
        row_long_inverse(g, arrived(1), rowm.at[3], row_s.at[0])
        if g == 1:
            loop(16, lambda t: keep(grid_u, t, row_short_inverse(t, row_s.at[0])))
        finish(2, g)
        row_long_inverse(g, arrived(2), rowm.at[2], row_s.at[1])
        if g == 1:
            loop(16, lambda t: keep(grid_v, t, row_short_inverse(t, row_s.at[1])))
        finish(3, g)
        row_long_inverse(g, arrived(3), rowm.at[2], row_s.at[2])

    def nonlinear(t):
        tiles = row_short_inverse(t, row_s.at[2])
        product = []
        for b in range(16):
            grid_wx[b, tile(t), :] = tiles[b]
            product.append(
                grid_u[b, tile(t), :] * tiles[b] + grid_v[b, tile(t), :] * grid_wy[b, tile(t), :])
        row_short_forward(t, product, row_s.at[0])

    loop(16, nonlinear)
    for g in both:
        row_long_forward(g, rowm.at[0], row_s.at[0], sends.at[4])
        start(4, g)
    table_copy(1).wait()

    wait_before(recv_sem)
    for g in both:
        forward_columns(g, 10, put(next_start))

    for g in both:
        first = 0 if g == 0 else CHUNK[0]
        ky = waves[0, first : first + CHUNK[g], :] + waves[1, first : first + CHUNK[g], :] * me.astype(F32)

        def put_end(rows, c, value, ky=ky):
            re, im = halves(w_spec, rows)
            decay, nlf, dx = decay_t[rows, :], nlf_t[rows, :], dx_t[rows, :]
            forced = (dx == 0.0) & (nlf > 0.0) & (ky == float(FORCING_WAVE))
            force = jnp.where(forced, TIME_STEP * FORCE_AMP * (N * N / 2.0) * decay, 0.0)
            end_re = decay * re - nlf * value[:, 0:LANES] + force
            end_im = decay * im - nlf * value[:, LANES : 2 * LANES]
            e_spec[rows, :] = two(end_re, end_im)
            next_re, next_im = halves(next_start, rows)
            adj[rows, :] = two(end_re - next_re, end_im - next_im)

        def weight_hat(rows):
            re, im = halves(adj, rows)
            nlf = nlf_t[rows, :]
            return two(nlf * re, nlf * im)

        finish(4, g)
        forward_columns(g, 4, put_end)
        inverse_columns(g, 5, weight_hat)
    seg_copy().start()

    for g in both:
        finish(5, g)
        row_long_inverse(g, arrived(5), rowm.at[2], row_s.at[0])

    def weighted(t):
        tiles = row_short_inverse(t, row_s.at[0])
        keep(grid_a, t, tiles)
        row_short_forward(t, [tiles[b] * grid_u[b, tile(t), :] for b in range(16)], row_s.at[1])

    def product(ref, scratch):
        def step(t):
            tiles = [grid_a[b, tile(t), :] * ref[b, tile(t), :] for b in range(16)]
            row_short_forward(t, tiles, scratch)
        return step

    loop(16, weighted)
    for g in both:
        row_long_forward(g, rowm.at[0], row_s.at[1], sends.at[6])
        start(6, g)
    for f, ref, mat in ((7, grid_wx, 1), (8, grid_wy, 0)):
        loop(16, product(ref, row_s.at[0]))
        for g in both:
            row_long_forward(g, rowm.at[mat], row_s.at[0], sends.at[f])
            start(f, g)
    loop(16, product(grid_v, row_s.at[0]))
    for g in both:
        row_long_forward(g, rowm.at[1], row_s.at[0], local_b)

    seg_copy().wait_recv()

    def make_residual(g):
        def step(c):
            rows = chunk(g, c)
            prev_re, prev_im = halves(prev_end, rows)
            re, im = halves(w_spec, rows)
            res_re, res_im = prev_re - re, prev_im - im
            prev_end[rows, :] = two(res_re, res_im)
            adj_re, adj_im = halves(adj, rows)
            decay = decay_t[rows, :]
            adj[rows, :] = two(decay * adj_re - res_re, decay * adj_im - res_im)
        return step

    for g in both:
        loop(4, make_residual(g), 1)

    slots = slot_table()

    def write_residual(k, mirror, flip):
        for part in range(2):
            lanes = slice(part * LANES, (part + 1) * LANES)
            for j in range(8):
                direct = prev_end[tile_rows(k, j), lanes]
                mirrored = prev_end[tile_rows(mirror, j), lanes]
                if part:
                    mirrored = -mirrored
                for h in range(2):
                    to = int(slots[j, 4 * h])
                    flat[part, 0, pl.ds(to, 4, stride=16), :] = direct[4 * h : 4 * h + 4]
                    flat[part, 1, pl.ds(64 + to, 4, stride=16), :] = mirrored[4 * h : 4 * h + 4]
            extra = prev_end[tile_rows(k, 8), lanes]
            flat[part, 0, 64:72, :] = jnp.where(first_mask, extra, 0.0)
            flat[part, 1, 64:72, :] = jnp.where(first_mask, 0.0, flat[part, 1, 64:72, :])
            high, low = split(jnp.concatenate([flat[part, 0], flat[part, 1]], axis=1))
            contract = (((1,), (1,)), ((), ()))
            result = lax.dot_general(flip, high, contract, preferred_element_type=F32)
            result = result + lax.dot_general(flip, low, contract, preferred_element_type=F32)
            resid_v[part, :, k, :] = result

    write_residual(0, 0, flips[0])
    loop(15, lambda i: write_residual(i + 1, 15 - i, flips[1]), 1)
    resid_copy = pltpu.make_async_copy(resid_v, resid, out_sem.at[0])
    resid_copy.start()

    def add_a(rows, c, value):
        re, im = halves(adj, rows)
        dx = dx_t[rows, :]
        adj[rows, :] = two(re - dx * value[:, LANES : 2 * LANES], im + dx * value[:, 0:LANES])

    def add_c(rows, c, value):
        re, im = halves(adj, rows)
        linv = linv_t[rows, :]
        adj[rows, :] = two(re + linv * value[:, 0:LANES], im + linv * value[:, LANES : 2 * LANES])

    def add_d(rows, c, value):
        re, im = halves(adj, rows)
        factor = linv_t[rows, :] * dx_t[rows, :]
        adj[rows, :] = two(
            re + factor * value[:, LANES : 2 * LANES], im - factor * value[:, 0:LANES])

    for f, emit in ((6, add_a), (7, add_c), (8, add_d)):
        for g in both:
            finish(f, g)
            forward_columns(g, f, emit)
            if f == 8:
                inverse_columns(g, 9, lambda rows: adj[rows, :])

    def total(j):
        return (recvs[9, :, j] + local_b[:, j]).reshape(256, LANES)

    for g in both:
        finish(9, g)
        row_long_inverse(g, total, rowm.at[2], row_s.at[0])
    loop(16, lambda t: keep(grid_a, t, row_short_inverse(t, row_s.at[0])))
    for b in range(16):
        grad_v[:, b * LANES : (b + 1) * LANES] = grid_a[b].T
    grad_copy = pltpu.make_async_copy(grad_v, grad, out_sem.at[1])
    grad_copy.start()
    for f in range(10):
        for g in both:
            finish_send(f, g)
    wait_before(send_sem)
    seg_copy().wait_send()
    resid_copy.wait()
    grad_copy.wait()


def body(vorticity):
    col_mats, twiddle = col_tables()
    vmem = pl.BlockSpec(memory_space=pltpu.VMEM)
    hbm = pl.BlockSpec(memory_space=pl.ANY)
    slab = (16, 8, 2, 8, LANES)
    grid = pltpu.VMEM((16, LANES, LANES), F32)
    spectrum = pltpu.VMEM((ALL_ROWS, 2 * LANES), F32)
    factor = pltpu.VMEM((ALL_ROWS, LANES), F32)
    outs = ((LANES, N), (2, LANES, 16, LANES))
    gradient, residual = pl.pallas_call(
        kernel,
        out_shape=tuple(jax.ShapeDtypeStruct(shape, F32) for shape in outs),
        in_specs=[vmem, hbm, vmem, vmem, vmem, vmem],
        out_specs=(hbm, hbm),
        scratch_shapes=[
            pltpu.VMEM((4, 2, 8, 256, 256), BF16),
            grid, grid, grid, grid, grid,
            pltpu.VMEM((10,) + slab, F32),
            pltpu.VMEM((11,) + slab, F32),
            pltpu.VMEM(slab, F32),
            pltpu.VMEM((3, 8, 256, LANES), F32),
            spectrum, spectrum, spectrum, spectrum, spectrum, spectrum,
            factor, factor, factor, factor,
            pltpu.VMEM((2, 2, LANES, LANES), F32),
            pltpu.VMEM(outs[0], F32),
            pltpu.VMEM(outs[1], F32),
            pltpu.SemaphoreType.DMA((4,)),
            pltpu.SemaphoreType.DMA((2,)),
            pltpu.SemaphoreType.DMA((10, 2)),
            pltpu.SemaphoreType.DMA((11, 2)),
            pltpu.SemaphoreType.DMA((11, 2)),
            pltpu.SemaphoreType.DMA,
            pltpu.SemaphoreType.DMA,
        ],
        compiler_params=pltpu.CompilerParams(
            collective_id=0, has_side_effects=True, vmem_limit_bytes=62 * 2**20
        ),
        name="orbit_gradient",
    )(vorticity[0], jnp.asarray(row_tables()), jnp.asarray(col_mats), jnp.asarray(twiddle),
      jnp.asarray(flip_tables()), jnp.asarray(wave_table()))
    return gradient[None], residual.reshape(1, 2, N, LANES)


def solution(mesh):
    return jax.shard_map(
        body,
        mesh=mesh,
        in_specs=(P("seg", "space", None),),
        out_specs=(P("seg", "space", None), P("seg", None, None, "space")),
        check_vma=False,
    )
```

time: 227 us -> 192 us (0.85)
  the two profiles are of different devices: /device:TPU:33 before, /device:TPU:37 now
where the time goes in v2:
time: 192 us
  Pallas kernels  188 us (98%)
  local copies, waits for them, and re-layouts  3.77 us (2%)
    pallas_call x1, Pallas kernels, body(): pl.pallas_call(kernel, out_shape=tuple((jax.ShapeDtypeStruct(shape, F32)...  188 us

profile of v2, /device:TPU:37, one launch (start us, length us, event | category | flops | bytes accessed | tf_op | source)
XLA Modules:
  0.0 192.1 jit_solution(15008213944630304728)
XLA Ops:
  0.6 187.7 %orbit_gradient.1 = (f32[128,2048]{1,0:T(8,128)}, f32[2,128,16,128]{3,2,1,0:T(8,128)}) custom-call(f32[128,2048]{1,0:T(8,128)} %bitcast.4, bf16[4,2,8,256,256]{4,3,2,1,0:T(8,128)(2,1)} %constant.10.clone.row_hbm, bf16[2,2,256,256]{3,2,1,0:T(8,128)(2,1)} %constant.11.clone.col_mats, f32[16,2,8,128]{3,2,1,0:T(8,128)} %constant.12.clone.twiddle, ...), custom_call_target="tpu_custom_call" | custom-call | tf_op jit(solution)/shard_map/orbit_gradient/pallas_call | solution.py:753
  188.4 0.0 copy-start
  188.4 2.4 %copy.10 = f32[1,128,2048]{2,1,0:T(8,128)} copy(f32[1,128,2048]{2,1,0:T(8,128)} %bitcast.5) | data formatting | bytes 2097152
  190.8 0.0 copy-done
  190.8 1.3 copy.11
Async XLA Ops:
  188.4 2.5 %copy-start = (f32[2,128,16,128]{3,2,1,0:T(8,128)S(1)}, f32[2,128,16,128]{3,2,1,0:T(8,128)}, u32[]{:S(2)}) copy-start(f32[2,128,16,128]{3,2,1,0:T(8,128)} %get-tuple-element.5) | copy-start | bytes 6291460

commit v3 on v2

--- a/solution.py
+++ b/solution.py
@@ -362,9 +362,9 @@
     vort, row_hbm, col_mats, twiddle, flips, waves,
     grad, resid,
     rowm, grid_a, grid_u, grid_v, grid_wx, grid_wy, sends, recvs, local_b,
-    row_s, col_s, w_spec, e_spec, adj, next_start, prev_end,
+    row_s, col_s, w_spec, previous, adj, next_start, residual,
     dx_t, linv_t, decay_t, nlf_t, flat, grad_v, resid_v,
-    table_sem, out_sem, own_sem, send_sem, recv_sem, seg_send, seg_recv,
+    table_sem, out_sem, own_sem, send_sem, recv_sem,
 ):
     me = lax.axis_index("space")
     seg = lax.axis_index("seg")
@@ -450,20 +450,32 @@
         else:
             wait_bytes(f, g, send_sem, 15)
 
-    def start_before():
+    side = {10: (0, before), 11: (0, after), 12: (4, after)}
+
+    def start_side(f):
+        source, s = side[f]
+
+        def one(p):
+            pltpu.make_async_remote_copy(
+                src_ref=sends.at[source, p], dst_ref=recvs.at[f, me],
+                send_sem=send_sem.at[f, 0], recv_sem=recv_sem.at[f, 0],
+                device_id={"seg": s, "space": p}, device_id_type=MESH).start()
+
         for p in [me] + others:
-            pltpu.make_async_remote_copy(
-                src_ref=sends.at[0, p], dst_ref=recvs.at[10, me],
-                send_sem=send_sem.at[10, 0], recv_sem=recv_sem.at[10, 0],
-                device_id={"seg": before, "space": p}, device_id_type=MESH).start()
-
-    def wait_before(sem):
-        pltpu.make_async_copy(sends.at[0], recvs.at[10], sem.at[10, 0]).wait()
-
-    def seg_copy():
-        return pltpu.make_async_remote_copy(
-            src_ref=e_spec, dst_ref=prev_end, send_sem=seg_send, recv_sem=seg_recv,
-            device_id={"seg": after}, device_id_type=MESH)
+            if f == 12:
+                pl.when(p < KEPT)(functools.partial(one, p))
+            else:
+                one(p)
+
+    def wait_side(f, sem, count=16):
+        pltpu.make_async_copy(
+            sends.at[side[f][0], pl.ds(0, count)], recvs.at[f, pl.ds(0, count)], sem.at[f, 0]).wait()
+
+    def finish_side(f):
+        if f == 12:
+            pl.when(me < KEPT)(lambda: wait_side(f, recv_sem))
+        else:
+            wait_side(f, recv_sem)
 
     for b in range(16):
         grid_a[b] = vort[:, b * LANES : (b + 1) * LANES].T
@@ -517,7 +529,11 @@
 
     @pl.when(me >= KEPT)
     def _():
-        loop(16, lambda b: recvs.__setitem__((4, b), jnp.zeros((8, 2, 8, LANES), F32)), 1)
+        def clear(b):
+            recvs[4, b] = jnp.zeros((8, 2, 8, LANES), F32)
+            recvs[12, b] = jnp.zeros((8, 2, 8, LANES), F32)
+
+        loop(16, clear, 1)
 
     loop(16 - KEPT, lambda b: zero_columns(b + KEPT), 1)
     flat[...] = jnp.zeros_like(flat)
@@ -561,7 +577,7 @@
         inverse_columns(g, 1, psi_hat)
         inverse_columns(g, 2, v_hat)
         inverse_columns(g, 3, wx_hat)
-    start_before()
+    start_side(10)
 
     table_copy(3).wait()
     for g in both:
@@ -594,36 +610,44 @@
     for g in both:
         row_long_forward(g, rowm.at[0], row_s.at[0], sends.at[4])
         start(4, g)
+    start_side(12)
     table_copy(1).wait()
 
-    wait_before(recv_sem)
+    finish_side(10)
     for g in both:
         forward_columns(g, 10, put(next_start))
 
-    for g in both:
-        first = 0 if g == 0 else CHUNK[0]
-        ky = waves[0, first : first + CHUNK[g], :] + waves[1, first : first + CHUNK[g], :] * me.astype(F32)
-
-        def put_end(rows, c, value, ky=ky):
-            re, im = halves(w_spec, rows)
-            decay, nlf, dx = decay_t[rows, :], nlf_t[rows, :], dx_t[rows, :]
-            forced = (dx == 0.0) & (nlf > 0.0) & (ky == float(FORCING_WAVE))
-            force = jnp.where(forced, TIME_STEP * FORCE_AMP * (N * N / 2.0) * decay, 0.0)
-            end_re = decay * re - nlf * value[:, 0:LANES] + force
-            end_im = decay * im - nlf * value[:, LANES : 2 * LANES]
-            e_spec[rows, :] = two(end_re, end_im)
+    def own_ky(g):
+        rows = slice(0, CHUNK[0]) if g == 0 else slice(CHUNK[0], CHUNK[0] + CHUNK[1])
+        return waves[0, rows, :] + waves[1, rows, :] * me.astype(F32)
+
+    def end_of(g, rows, ref, value):
+        re, im = halves(ref, rows)
+        decay, nlf = decay_t[rows, :], nlf_t[rows, :]
+        forced = (dx_t[rows, :] == 0.0) & (nlf > 0.0) & (own_ky(g) == float(FORCING_WAVE))
+        force = jnp.where(forced, TIME_STEP * FORCE_AMP * (N * N / 2.0) * decay, 0.0)
+        return (
+            decay * re - nlf * value[:, 0:LANES] + force,
+            decay * im - nlf * value[:, LANES : 2 * LANES],
+        )
+
+    def put_adjoint(g):
+        def emit(rows, c, value):
+            end_re, end_im = end_of(g, rows, w_spec, value)
             next_re, next_im = halves(next_start, rows)
             adj[rows, :] = two(end_re - next_re, end_im - next_im)
-
-        def weight_hat(rows):
-            re, im = halves(adj, rows)
-            nlf = nlf_t[rows, :]
-            return two(nlf * re, nlf * im)
-
+        return emit
+
+    def weight_hat(rows):
+        re, im = halves(adj, rows)
+        nlf = nlf_t[rows, :]
+        return two(nlf * re, nlf * im)
+
+    for g in both:
         finish(4, g)
-        forward_columns(g, 4, put_end)
+        forward_columns(g, 4, put_adjoint(g))
         inverse_columns(g, 5, weight_hat)
-    seg_copy().start()
+    start_side(11)
 
     for g in both:
         finish(5, g)
@@ -653,22 +677,23 @@
     for g in both:
         row_long_forward(g, rowm.at[1], row_s.at[0], local_b)
 
-    seg_copy().wait_recv()
-
-    def make_residual(g):
-        def step(c):
-            rows = chunk(g, c)
-            prev_re, prev_im = halves(prev_end, rows)
+    def put_residual(g):
+        def emit(rows, c, value):
+            prev_re, prev_im = end_of(g, rows, previous, value)
             re, im = halves(w_spec, rows)
             res_re, res_im = prev_re - re, prev_im - im
-            prev_end[rows, :] = two(res_re, res_im)
+            residual[rows, :] = two(res_re, res_im)
             adj_re, adj_im = halves(adj, rows)
             decay = decay_t[rows, :]
             adj[rows, :] = two(decay * adj_re - res_re, decay * adj_im - res_im)
-        return step
-
-    for g in both:
-        loop(4, make_residual(g), 1)
+        return emit
+
+    finish_side(11)
+    for g in both:
+        forward_columns(g, 11, put(previous))
+    finish_side(12)
+    for g in both:
+        forward_columns(g, 12, put_residual(g))
 
     slots = slot_table()
 
@@ -676,15 +701,15 @@
         for part in range(2):
             lanes = slice(part * LANES, (part + 1) * LANES)
             for j in range(8):
-                direct = prev_end[tile_rows(k, j), lanes]
-                mirrored = prev_end[tile_rows(mirror, j), lanes]
+                direct = residual[tile_rows(k, j), lanes]
+                mirrored = residual[tile_rows(mirror, j), lanes]
                 if part:
                     mirrored = -mirrored
                 for h in range(2):
                     to = int(slots[j, 4 * h])
                     flat[part, 0, pl.ds(to, 4, stride=16), :] = direct[4 * h : 4 * h + 4]
                     flat[part, 1, pl.ds(64 + to, 4, stride=16), :] = mirrored[4 * h : 4 * h + 4]
-            extra = prev_end[tile_rows(k, 8), lanes]
+            extra = residual[tile_rows(k, 8), lanes]
             flat[part, 0, 64:72, :] = jnp.where(first_mask, extra, 0.0)
             flat[part, 1, 64:72, :] = jnp.where(first_mask, 0.0, flat[part, 1, 64:72, :])
             high, low = split(jnp.concatenate([flat[part, 0], flat[part, 1]], axis=1))
@@ -735,8 +760,9 @@
     for f in range(10):
         for g in both:
             finish_send(f, g)
-    wait_before(send_sem)
-    seg_copy().wait_send()
+    wait_side(10, send_sem)
+    wait_side(11, send_sem)
+    wait_side(12, send_sem, KEPT)
     resid_copy.wait()
     grad_copy.wait()
 
@@ -759,7 +785,7 @@
             pltpu.VMEM((4, 2, 8, 256, 256), BF16),
             grid, grid, grid, grid, grid,
             pltpu.VMEM((10,) + slab, F32),
-            pltpu.VMEM((11,) + slab, F32),
+            pltpu.VMEM((13,) + slab, F32),
             pltpu.VMEM(slab, F32),
             pltpu.VMEM((3, 8, 256, LANES), F32),
             spectrum, spectrum, spectrum, spectrum, spectrum, spectrum,
@@ -770,10 +796,8 @@
             pltpu.SemaphoreType.DMA((4,)),
             pltpu.SemaphoreType.DMA((2,)),
             pltpu.SemaphoreType.DMA((10, 2)),
-            pltpu.SemaphoreType.DMA((11, 2)),
-            pltpu.SemaphoreType.DMA((11, 2)),
-            pltpu.SemaphoreType.DMA,
-            pltpu.SemaphoreType.DMA,
+            pltpu.SemaphoreType.DMA((13, 2)),
+            pltpu.SemaphoreType.DMA((13, 2)),
         ],
         compiler_params=pltpu.CompilerParams(
             collective_id=0, has_side_effects=True, vmem_limit_bytes=62 * 2**20

time: 192 us -> 181 us (0.943)
  the two profiles are of different devices: /device:TPU:37 before, /device:TPU:1 now
where the time goes in v3:
time: 181 us; the launch traced here: 180 us
  Pallas kernels  176 us (97%)
  local copies, waits for them, and re-layouts  3.77 us (2%)
    pallas_call x1, Pallas kernels, body(): pl.pallas_call(kernel, out_shape=tuple((jax.ShapeDtypeStruct(shape, F32)...  176 us
    unnamed x4, local copies, waits for them, and re-layouts  3.77 us

profile of v3, /device:TPU:1, one launch (start us, length us, event | category | flops | bytes accessed | tf_op | source)
XLA Modules:
  0.0 180.0 jit_solution(6850145825734970958)
XLA Ops:
  0.6 175.6 %orbit_gradient.1 = (f32[128,2048]{1,0:T(8,128)}, f32[2,128,16,128]{3,2,1,0:T(8,128)}) custom-call(f32[128,2048]{1,0:T(8,128)} %bitcast.4, bf16[4,2,8,256,256]{4,3,2,1,0:T(8,128)(2,1)} %constant.10.clone.row_hbm, bf16[2,2,256,256]{3,2,1,0:T(8,128)(2,1)} %constant.11.clone.col_mats, f32[16,2,8,128]{3,2,1,0:T(8,128)} %constant.12.clone.twiddle, ...), custom_call_target="tpu_custom_call" | custom-call | tf_op jit(solution)/shard_map/orbit_gradient/pallas_call | solution.py:779
  176.2 0.0 copy-start
  176.2 2.4 %copy.10 = f32[1,128,2048]{2,1,0:T(8,128)} copy(f32[1,128,2048]{2,1,0:T(8,128)} %bitcast.5) | data formatting | bytes 2097152
  178.7 0.0 copy-done
  178.7 1.3 copy.11
Async XLA Ops:
  176.2 2.5 %copy-start = (f32[2,128,16,128]{3,2,1,0:T(8,128)S(1)}, f32[2,128,16,128]{3,2,1,0:T(8,128)}, u32[]{:S(2)}) copy-start(f32[2,128,16,128]{3,2,1,0:T(8,128)} %get-tuple-element.5) | copy-start | bytes 6291460

commit v4 on v3

--- a/solution.py
+++ b/solution.py
@@ -577,7 +577,6 @@
         inverse_columns(g, 1, psi_hat)
         inverse_columns(g, 2, v_hat)
         inverse_columns(g, 3, wx_hat)
-    start_side(10)
 
     table_copy(3).wait()
     for g in both:
@@ -594,6 +593,9 @@
         row_long_inverse(g, arrived(2), rowm.at[2], row_s.at[1])
         if g == 1:
             loop(16, lambda t: keep(grid_v, t, row_short_inverse(t, row_s.at[1])))
+        if g == 1:
+            finish_send(3, 1)
+            start_side(10)
         finish(3, g)
         row_long_inverse(g, arrived(3), rowm.at[2], row_s.at[2])
 
@@ -759,7 +761,8 @@
     grad_copy.start()
     for f in range(10):
         for g in both:
-            finish_send(f, g)
+            if (f, g) != (3, 1):
+                finish_send(f, g)
     wait_side(10, send_sem)
     wait_side(11, send_sem)
     wait_side(12, send_sem, KEPT)

time: 181 us -> 178 us (0.983)
  Pallas kernels: 176 us -> 173 us
    pallas_call x1, Pallas kernels: 176 us -> 173 us  [body(): pl.pallas_call(kernel, out_shape=tuple((jax.ShapeDtypeStruct(shape, F32)...]
where the time goes in v4:
time: 178 us
  Pallas kernels  173 us (97%)
  local copies, waits for them, and re-layouts  3.77 us (2%)
    pallas_call x1, Pallas kernels, body(): pl.pallas_call(kernel, out_shape=tuple((jax.ShapeDtypeStruct(shape, F32)...  173 us
    unnamed x4, local copies, waits for them, and re-layouts  3.77 us

profile of v4, /device:TPU:1, one launch (start us, length us, event | category | flops | bytes accessed | tf_op | source)
XLA Modules:
  0.0 177.8 jit_solution(8098221725027666927)
XLA Ops:
  0.6 173.4 %orbit_gradient.1 = (f32[128,2048]{1,0:T(8,128)}, f32[2,128,16,128]{3,2,1,0:T(8,128)}) custom-call(f32[128,2048]{1,0:T(8,128)} %bitcast.4, bf16[4,2,8,256,256]{4,3,2,1,0:T(8,128)(2,1)} %constant.10.clone.row_hbm, bf16[2,2,256,256]{3,2,1,0:T(8,128)(2,1)} %constant.11.clone.col_mats, f32[16,2,8,128]{3,2,1,0:T(8,128)} %constant.12.clone.twiddle, ...), custom_call_target="tpu_custom_call" | custom-call | tf_op jit(solution)/shard_map/orbit_gradient/pallas_call | solution.py:782
  174.0 0.0 copy-start
  174.0 2.4 %copy.10 = f32[1,128,2048]{2,1,0:T(8,128)} copy(f32[1,128,2048]{2,1,0:T(8,128)} %bitcast.5) | data formatting | bytes 2097152
  176.5 0.0 copy-done
  176.5 1.3 copy.11
Async XLA Ops:
  174.0 2.5 %copy-start = (f32[2,128,16,128]{3,2,1,0:T(8,128)S(1)}, f32[2,128,16,128]{3,2,1,0:T(8,128)}, u32[]{:S(2)}) copy-start(f32[2,128,16,128]{3,2,1,0:T(8,128)} %get-tuple-element.5) | copy-start | bytes 6291460

commit v5 on v4

--- a/solution.py
+++ b/solution.py
@@ -452,7 +452,7 @@
 
     side = {10: (0, before), 11: (0, after), 12: (4, after)}
 
-    def start_side(f):
+    def start_side(f, first=0, last=16):
         source, s = side[f]
 
         def one(p):
@@ -461,7 +461,7 @@
                 send_sem=send_sem.at[f, 0], recv_sem=recv_sem.at[f, 0],
                 device_id={"seg": s, "space": p}, device_id_type=MESH).start()
 
-        for p in [me] + others:
+        for p in ([me] + others)[first:last]:
             if f == 12:
                 pl.when(p < KEPT)(functools.partial(one, p))
             else:
@@ -596,6 +596,7 @@
         if g == 1:
             finish_send(3, 1)
             start_side(10)
+            start_side(11, 0, 8)
         finish(3, g)
         row_long_inverse(g, arrived(3), rowm.at[2], row_s.at[2])
 
@@ -649,7 +650,7 @@
         finish(4, g)
         forward_columns(g, 4, put_adjoint(g))
         inverse_columns(g, 5, weight_hat)
-    start_side(11)
+    start_side(11, 8, 16)
 
     for g in both:
         finish(5, g)

time: 178 us -> 175 us (0.983)
  Pallas kernels: 173 us -> 169 us
    pallas_call x1, Pallas kernels: 173 us -> 169 us  [body(): pl.pallas_call(kernel, out_shape=tuple((jax.ShapeDtypeStruct(shape, F32)...]
where the time goes in v5:
time: 175 us; the launch traced here: 174 us
  Pallas kernels  169 us (97%)
  local copies, waits for them, and re-layouts  3.77 us (2%)
    pallas_call x1, Pallas kernels, body(): pl.pallas_call(kernel, out_shape=tuple((jax.ShapeDtypeStruct(shape, F32)...  169 us
    unnamed x4, local copies, waits for them, and re-layouts  3.77 us

profile of v5, /device:TPU:1, one launch (start us, length us, event | category | flops | bytes accessed | tf_op | source)
XLA Modules:
  0.0 173.9 jit_solution(12309649464682389438)
XLA Ops:
  0.6 169.5 %orbit_gradient.1 = (f32[128,2048]{1,0:T(8,128)}, f32[2,128,16,128]{3,2,1,0:T(8,128)}) custom-call(f32[128,2048]{1,0:T(8,128)} %bitcast.4, bf16[4,2,8,256,256]{4,3,2,1,0:T(8,128)(2,1)} %constant.10.clone.row_hbm, bf16[2,2,256,256]{3,2,1,0:T(8,128)(2,1)} %constant.11.clone.col_mats, f32[16,2,8,128]{3,2,1,0:T(8,128)} %constant.12.clone.twiddle, ...), custom_call_target="tpu_custom_call" | custom-call | tf_op jit(solution)/shard_map/orbit_gradient/pallas_call | solution.py:783
  170.1 0.0 copy-start
  170.1 2.4 %copy.10 = f32[1,128,2048]{2,1,0:T(8,128)} copy(f32[1,128,2048]{2,1,0:T(8,128)} %bitcast.5) | data formatting | bytes 2097152
  172.6 0.0 copy-done
  172.6 1.3 copy.11
Async XLA Ops:
  170.1 2.5 %copy-start = (f32[2,128,16,128]{3,2,1,0:T(8,128)S(1)}, f32[2,128,16,128]{3,2,1,0:T(8,128)}, u32[]{:S(2)}) copy-start(f32[2,128,16,128]{3,2,1,0:T(8,128)} %get-tuple-element.5) | copy-start | bytes 6291460
